TPU v7x, 512 devices: a whole 4x4x16 slice. The times are simulated.
512 devices in a mesh: dp: 4 (over x), ctx: 32 (over z, core), head: 4 (over y).
Axes of the slice: x: 4, y: 4, z: 16, core: 2. Of those that a mesh axis runs over, the one named last changes fastest.
Arguments:
- tokens: bfloat16 [32768, 4096], P(('dp', 'ctx'), 'head'), parts along dimension 0, may hold values from -6 to 6
- query: bfloat16 [32768, 2048], P(('dp', 'ctx'), 'head'), parts along dimension 0, may hold values from -109 to 109, as said below
- w_key: bfloat16 [4096, 512], P(None, 'head'), may hold values from -0.09375 to 0.09375
- w_value: bfloat16 [4096, 512], P(None, 'head'), may hold values from -0.09375 to 0.09375
- doc_lengths: int32 [64], P('dp'), parts along dimension 0, may hold values from 1 to 2048, 8192 in all
- balance: int32 [128, 32], P('dp'), parts along dimension 0, may hold values from 0 to 31, each once within a row
Outputs:
- attended: bfloat16 [32768, 2048], P(('dp', 'ctx'), 'head'), parts along dimension 0
There are 4 independent parts, one for each index of `dp`. A program takes and returns all parts, laid end to end along the dimension named above; an argument that names none is the same for every part. Nothing has to cross between parts.
Inputs may be any that keep to these rules, and one draw needn't show every extreme that they name: `query`: rows scale the draw independently.
All inputs are finite; a program needn't handle non-finite values.
Results may differ from a plain program's by a relative error of at most 0.012.
The roundings to bfloat16 on the way count: a program that leaves them out, or rounds other values in their place, can miss the bound.
Values may be sent and summed in bfloat16 or wider, within the bound.
A program may use at most 64 MiB of HBM per device.

v0:
```python
import jax
import jax.numpy as jnp
from jax import lax
from jax.sharding import PartitionSpec as P

HD = 128


rope_base = 500000.0
masked = -1e30


def from_behind(block, axis, distance):
    devices = range(lax.axis_size(axis))
    route = [((i - distance) % len(devices), i) for i in devices]
    return lax.ppermute(block, axis, route)


def rotate(keys_raw, positions):
    half = HD // 2
    freq = rope_base ** (-(jnp.arange(half, dtype=jnp.float32) * 2.0 / HD))
    angle = positions.astype(jnp.float32)[:, None] * freq[None, :]
    cosine = jnp.cos(angle)[:, None, :]
    sine = jnp.sin(angle)[:, None, :]
    first = keys_raw[..., :half]
    second = keys_raw[..., half:]
    return jnp.concatenate(
        [first * cosine - second * sine, second * cosine + first * sine], axis=-1
    )


def local(tokens, query, w_key, w_value, doc_lengths, balance):
    nctx = lax.axis_size("ctx")
    me = lax.axis_index("ctx")
    rows = tokens.shape[0]
    brow = rows // nctx
    inverse = jnp.argsort(balance, axis=1)
    flat_inverse = inverse.reshape(-1)
    mine = lax.dynamic_index_in_dim(inverse, me, 0, keepdims=False)

    def shard_positions(shard):
        return shard * rows + jnp.arange(rows, dtype=jnp.int32)

    bounds = jnp.cumsum(doc_lengths)

    def doc_of(positions):
        return jnp.sum((positions[:, None] >= bounds[None, :]).astype(jnp.int32), axis=1)

    kv_width = w_key.shape[1]
    piece = lax.all_gather(tokens, "head", axis=1, tiled=True)
    keys_raw = jnp.dot(piece, w_key, preferred_element_type=jnp.float32)
    values_raw = jnp.dot(piece, w_value, preferred_element_type=jnp.float32)
    own_pos = shard_positions(me)
    kvl = kv_width // HD
    keys = (
        rotate(keys_raw.reshape(rows, kvl, HD), own_pos)
        .reshape(rows, kv_width)
        .astype(jnp.bfloat16)
    )
    both = jnp.concatenate([keys, values_raw.astype(jnp.bfloat16)], axis=1)
    group = query.shape[1] // kv_width
    scale = 1.0 / HD**0.5

    def make_attend(qrows, qpos):
        qheads = qrows.reshape(rows, kvl, group, HD)
        qdoc = doc_of(qpos)

        def attend(state, block, kpos):
            top, total, acc = state
            khead = block[:, :kv_width].reshape(-1, kvl, HD)
            vhead = block[:, kv_width:].reshape(-1, kvl, HD)
            scores = (
                jnp.einsum("qcgd,kcd->cgqk", qheads, khead, preferred_element_type=jnp.float32)
                * scale
            )
            allowed = (
                (kpos[None, :] >= 0)
                & (kpos[None, :] <= qpos[:, None])
                & (doc_of(kpos)[None, :] == qdoc[:, None])
            )
            scores = jnp.where(allowed, scores, masked)
            new_top = jnp.maximum(top, jnp.max(scores, axis=-1))
            weights = jnp.where(allowed, jnp.exp(scores - new_top[..., None]), 0.0)
            keep = jnp.exp(top - new_top)
            total = total * keep + jnp.sum(weights, axis=-1)
            acc = acc * keep[..., None] + jnp.einsum(
                "cgqk,kcd->cgqd",
                weights.astype(jnp.bfloat16),
                vhead,
                preferred_element_type=jnp.float32,
            )
            return (new_top, total, acc)

        return attend

    init = (
        jnp.full((kvl, group, rows), masked, jnp.float32),
        jnp.zeros((kvl, group, rows), jnp.float32),
        jnp.zeros((kvl, group, rows, HD), jnp.float32),
    )
    shaped = query.reshape(nctx, brow, query.shape[1])
    local_q = lax.all_to_all(
        jnp.take(shaped, mine, axis=0).reshape(rows, query.shape[1]),
        "ctx",
        split_axis=0,
        concat_axis=0,
        tiled=True,
    )
    index = me * rows + jnp.arange(rows, dtype=jnp.int32)
    shard = index // rows
    inner = index % rows
    source = inner // brow
    offset = inner % brow
    block = jnp.take(flat_inverse, source * nctx + shard, axis=0)
    attend = make_attend(local_q, source * rows + block * brow + offset)
    state = attend(init, both, own_pos)

    def forward(step, carried):
        current, block = carried
        block = from_behind(block, "ctx", 1)
        return (attend(current, block, shard_positions((me - step - 1) % nctx)), block)

    state = lax.fori_loop(0, nctx - 1, forward, (state, both))[0]
    top, total, acc = state
    result = acc / total[..., None]
    return result.transpose(2, 0, 1, 3).reshape(rows, kvl * group * HD).astype(jnp.bfloat16)


def solution(mesh):
    placed = (
        P(("dp", "ctx"), "head"),
        P(("dp", "ctx"), "head"),
        P(None, "head"),
        P(None, "head"),
        P("dp"),
        P("dp", None),
    )
    return jax.shard_map(
        local, mesh=mesh, in_specs=placed, out_specs=P(("dp", "ctx"), "head"), check_vma=False
    )
```

profile of v0, /device:TPU:1, one launch (start us, length us, event | category | flops | bytes accessed | tf_op | source)
XLA Modules:
  0.0 271.8 jit_solution(6973395412434876853)
XLA Ops:
  11.4 16.7 %all-to-all-start = ((bf16[32,8,512]{2,1,0:T(8,128)(2,1)}), bf16[32,8,512]{2,1,0:T(8,128)(2,1)S(1)}, u32[]{:S(2)}, u32[]{:S(2)}) async-start(bf16[32,8,512]{2,1,0:T(8,128)(2,1)} %broadcast_select_fusion), calls=%async_computation | async-start | bytes 524288 | tf_op jit(solution)/shard_map/all_to_all | solution.py:102
  30.3 19.9 %all-to-all-done = bf16[32,8,512]{2,1,0:T(8,128)(2,1)S(1)} async-done(((bf16[32,8,512]{2,1,0:T(8,128)(2,1)}), bf16[32,8,512]{2,1,0:T(8,128)(2,1)S(1)}, u32[]{:S(2)}, u32[]{:S(2)}) %all-to-all-start) | async-done | bytes 262176 | tf_op jit(solution)/shard_map/all_to_all | solution.py:102
  50.4 3.0 %all-gather.2.cloned.1.call-done = bf16[256,4096]{1,0:T(8,128)(2,1)} async-done(((bf16[256,1024]{1,0:T(8,128)(2,1)}), bf16[256,4096]{1,0:T(8,128)(2,1)}) %all-gather.2.cloned.1.call-update) | async-done | bytes 2097168 | tf_op jit(solution)/shard_map/all_gather | solution.py:50
  58.3 205.4 %while.21 = (s32[]{:T(128)}, f32[1,4,256]{2,1,0:T(4,128)S(1)}, f32[1,4,256]{2,1,0:T(4,128)S(1)}, f32[1,4,256,128]{3,2,1,0:T(8,128)S(1)}, bf16[256,256]{1,0:T(8,1...) while((s32[]{:T(128)}, f32[1,4,256]{2,1,0:T(4,128)S(1)}, ...), condition=%wide.region_10.11_spmd, body=%wide.region_6.10_spmd.sunk | while | flops 137117200 | bytes 5709718 | solution.py:123
  77.0 3.6 %collective-permute-done = bf16[256,256]{1,0:T(8,128)(2,1)S(1)} collective-permute-done((bf16[256,256]{1,0:T(8,128)(2,1)S(1)}, bf16[256,256]{1,0:T(8,128)(2,1)S(1)}, u32[]{:S(2)}, u32[]{:S(2)}) %collective-permute-start) | collective-permute-done | bytes 131104 | tf_op jit(solution)/shard_map/while/body/eval_jaxpr/ppermute | solution.py:16
  82.6 4.8 %collective-permute-done = bf16[256,256]{1,0:T(8,128)(2,1)S(1)} collective-permute-done((bf16[256,256]{1,0:T(8,128)(2,1)S(1)}, bf16[256,256]{1,0:T(8,128)(2,1)S(1)}, u32[]{:S(2)}, u32[]{:S(2)}) %collective-permute-start) | collective-permute-done | bytes 131104 | tf_op jit(solution)/shard_map/while/body/eval_jaxpr/ppermute | solution.py:16
  88.8 5.3 %collective-permute-done = bf16[256,256]{1,0:T(8,128)(2,1)S(1)} collective-permute-done((bf16[256,256]{1,0:T(8,128)(2,1)S(1)}, bf16[256,256]{1,0:T(8,128)(2,1)S(1)}, u32[]{:S(2)}, u32[]{:S(2)}) %collective-permute-start) | collective-permute-done | bytes 131104 | tf_op jit(solution)/shard_map/while/body/eval_jaxpr/ppermute | solution.py:16
  95.5 5.3 %collective-permute-done = bf16[256,256]{1,0:T(8,128)(2,1)S(1)} collective-permute-done((bf16[256,256]{1,0:T(8,128)(2,1)S(1)}, bf16[256,256]{1,0:T(8,128)(2,1)S(1)}, u32[]{:S(2)}, u32[]{:S(2)}) %collective-permute-start) | collective-permute-done | bytes 131104 | tf_op jit(solution)/shard_map/while/body/eval_jaxpr/ppermute | solution.py:16
  102.3 5.3 %collective-permute-done = bf16[256,256]{1,0:T(8,128)(2,1)S(1)} collective-permute-done((bf16[256,256]{1,0:T(8,128)(2,1)S(1)}, bf16[256,256]{1,0:T(8,128)(2,1)S(1)}, u32[]{:S(2)}, u32[]{:S(2)}) %collective-permute-start) | collective-permute-done | bytes 131104 | tf_op jit(solution)/shard_map/while/body/eval_jaxpr/ppermute | solution.py:16
  109.0 5.3 %collective-permute-done = bf16[256,256]{1,0:T(8,128)(2,1)S(1)} collective-permute-done((bf16[256,256]{1,0:T(8,128)(2,1)S(1)}, bf16[256,256]{1,0:T(8,128)(2,1)S(1)}, u32[]{:S(2)}, u32[]{:S(2)}) %collective-permute-start) | collective-permute-done | bytes 131104 | tf_op jit(solution)/shard_map/while/body/eval_jaxpr/ppermute | solution.py:16
  115.8 5.3 %collective-permute-done = bf16[256,256]{1,0:T(8,128)(2,1)S(1)} collective-permute-done((bf16[256,256]{1,0:T(8,128)(2,1)S(1)}, bf16[256,256]{1,0:T(8,128)(2,1)S(1)}, u32[]{:S(2)}, u32[]{:S(2)}) %collective-permute-start) | collective-permute-done | bytes 131104 | tf_op jit(solution)/shard_map/while/body/eval_jaxpr/ppermute | solution.py:16
  122.5 5.3 %collective-permute-done = bf16[256,256]{1,0:T(8,128)(2,1)S(1)} collective-permute-done((bf16[256,256]{1,0:T(8,128)(2,1)S(1)}, bf16[256,256]{1,0:T(8,128)(2,1)S(1)}, u32[]{:S(2)}, u32[]{:S(2)}) %collective-permute-start) | collective-permute-done | bytes 131104 | tf_op jit(solution)/shard_map/while/body/eval_jaxpr/ppermute | solution.py:16
  129.3 5.3 %collective-permute-done = bf16[256,256]{1,0:T(8,128)(2,1)S(1)} collective-permute-done((bf16[256,256]{1,0:T(8,128)(2,1)S(1)}, bf16[256,256]{1,0:T(8,128)(2,1)S(1)}, u32[]{:S(2)}, u32[]{:S(2)}) %collective-permute-start) | collective-permute-done | bytes 131104 | tf_op jit(solution)/shard_map/while/body/eval_jaxpr/ppermute | solution.py:16
  136.0 5.3 %collective-permute-done = bf16[256,256]{1,0:T(8,128)(2,1)S(1)} collective-permute-done((bf16[256,256]{1,0:T(8,128)(2,1)S(1)}, bf16[256,256]{1,0:T(8,128)(2,1)S(1)}, u32[]{:S(2)}, u32[]{:S(2)}) %collective-permute-start) | collective-permute-done | bytes 131104 | tf_op jit(solution)/shard_map/while/body/eval_jaxpr/ppermute | solution.py:16
  142.7 5.3 %collective-permute-done = bf16[256,256]{1,0:T(8,128)(2,1)S(1)} collective-permute-done((bf16[256,256]{1,0:T(8,128)(2,1)S(1)}, bf16[256,256]{1,0:T(8,128)(2,1)S(1)}, u32[]{:S(2)}, u32[]{:S(2)}) %collective-permute-start) | collective-permute-done | bytes 131104 | tf_op jit(solution)/shard_map/while/body/eval_jaxpr/ppermute | solution.py:16
  149.5 5.3 %collective-permute-done = bf16[256,256]{1,0:T(8,128)(2,1)S(1)} collective-permute-done((bf16[256,256]{1,0:T(8,128)(2,1)S(1)}, bf16[256,256]{1,0:T(8,128)(2,1)S(1)}, u32[]{:S(2)}, u32[]{:S(2)}) %collective-permute-start) | collective-permute-done | bytes 131104 | tf_op jit(solution)/shard_map/while/body/eval_jaxpr/ppermute | solution.py:16
  156.2 5.3 %collective-permute-done = bf16[256,256]{1,0:T(8,128)(2,1)S(1)} collective-permute-done((bf16[256,256]{1,0:T(8,128)(2,1)S(1)}, bf16[256,256]{1,0:T(8,128)(2,1)S(1)}, u32[]{:S(2)}, u32[]{:S(2)}) %collective-permute-start) | collective-permute-done | bytes 131104 | tf_op jit(solution)/shard_map/while/body/eval_jaxpr/ppermute | solution.py:16
  163.0 5.3 %collective-permute-done = bf16[256,256]{1,0:T(8,128)(2,1)S(1)} collective-permute-done((bf16[256,256]{1,0:T(8,128)(2,1)S(1)}, bf16[256,256]{1,0:T(8,128)(2,1)S(1)}, u32[]{:S(2)}, u32[]{:S(2)}) %collective-permute-start) | collective-permute-done | bytes 131104 | tf_op jit(solution)/shard_map/while/body/eval_jaxpr/ppermute | solution.py:16
  169.7 5.3 %collective-permute-done = bf16[256,256]{1,0:T(8,128)(2,1)S(1)} collective-permute-done((bf16[256,256]{1,0:T(8,128)(2,1)S(1)}, bf16[256,256]{1,0:T(8,128)(2,1)S(1)}, u32[]{:S(2)}, u32[]{:S(2)}) %collective-permute-start) | collective-permute-done | bytes 131104 | tf_op jit(solution)/shard_map/while/body/eval_jaxpr/ppermute | solution.py:16
  176.4 5.3 %collective-permute-done = bf16[256,256]{1,0:T(8,128)(2,1)S(1)} collective-permute-done((bf16[256,256]{1,0:T(8,128)(2,1)S(1)}, bf16[256,256]{1,0:T(8,128)(2,1)S(1)}, u32[]{:S(2)}, u32[]{:S(2)}) %collective-permute-start) | collective-permute-done | bytes 131104 | tf_op jit(solution)/shard_map/while/body/eval_jaxpr/ppermute | solution.py:16
  183.2 5.3 %collective-permute-done = bf16[256,256]{1,0:T(8,128)(2,1)S(1)} collective-permute-done((bf16[256,256]{1,0:T(8,128)(2,1)S(1)}, bf16[256,256]{1,0:T(8,128)(2,1)S(1)}, u32[]{:S(2)}, u32[]{:S(2)}) %collective-permute-start) | collective-permute-done | bytes 131104 | tf_op jit(solution)/shard_map/while/body/eval_jaxpr/ppermute | solution.py:16
  189.9 5.3 %collective-permute-done = bf16[256,256]{1,0:T(8,128)(2,1)S(1)} collective-permute-done((bf16[256,256]{1,0:T(8,128)(2,1)S(1)}, bf16[256,256]{1,0:T(8,128)(2,1)S(1)}, u32[]{:S(2)}, u32[]{:S(2)}) %collective-permute-start) | collective-permute-done | bytes 131104 | tf_op jit(solution)/shard_map/while/body/eval_jaxpr/ppermute | solution.py:16
  196.7 5.3 %collective-permute-done = bf16[256,256]{1,0:T(8,128)(2,1)S(1)} collective-permute-done((bf16[256,256]{1,0:T(8,128)(2,1)S(1)}, bf16[256,256]{1,0:T(8,128)(2,1)S(1)}, u32[]{:S(2)}, u32[]{:S(2)}) %collective-permute-start) | collective-permute-done | bytes 131104 | tf_op jit(solution)/shard_map/while/body/eval_jaxpr/ppermute | solution.py:16
  203.4 5.3 %collective-permute-done = bf16[256,256]{1,0:T(8,128)(2,1)S(1)} collective-permute-done((bf16[256,256]{1,0:T(8,128)(2,1)S(1)}, bf16[256,256]{1,0:T(8,128)(2,1)S(1)}, u32[]{:S(2)}, u32[]{:S(2)}) %collective-permute-start) | collective-permute-done | bytes 131104 | tf_op jit(solution)/shard_map/while/body/eval_jaxpr/ppermute | solution.py:16
  210.2 5.3 %collective-permute-done = bf16[256,256]{1,0:T(8,128)(2,1)S(1)} collective-permute-done((bf16[256,256]{1,0:T(8,128)(2,1)S(1)}, bf16[256,256]{1,0:T(8,128)(2,1)S(1)}, u32[]{:S(2)}, u32[]{:S(2)}) %collective-permute-start) | collective-permute-done | bytes 131104 | tf_op jit(solution)/shard_map/while/body/eval_jaxpr/ppermute | solution.py:16
  216.9 5.3 %collective-permute-done = bf16[256,256]{1,0:T(8,128)(2,1)S(1)} collective-permute-done((bf16[256,256]{1,0:T(8,128)(2,1)S(1)}, bf16[256,256]{1,0:T(8,128)(2,1)S(1)}, u32[]{:S(2)}, u32[]{:S(2)}) %collective-permute-start) | collective-permute-done | bytes 131104 | tf_op jit(solution)/shard_map/while/body/eval_jaxpr/ppermute | solution.py:16
  223.6 5.3 %collective-permute-done = bf16[256,256]{1,0:T(8,128)(2,1)S(1)} collective-permute-done((bf16[256,256]{1,0:T(8,128)(2,1)S(1)}, bf16[256,256]{1,0:T(8,128)(2,1)S(1)}, u32[]{:S(2)}, u32[]{:S(2)}) %collective-permute-start) | collective-permute-done | bytes 131104 | tf_op jit(solution)/shard_map/while/body/eval_jaxpr/ppermute | solution.py:16
  230.4 5.3 %collective-permute-done = bf16[256,256]{1,0:T(8,128)(2,1)S(1)} collective-permute-done((bf16[256,256]{1,0:T(8,128)(2,1)S(1)}, bf16[256,256]{1,0:T(8,128)(2,1)S(1)}, u32[]{:S(2)}, u32[]{:S(2)}) %collective-permute-start) | collective-permute-done | bytes 131104 | tf_op jit(solution)/shard_map/while/body/eval_jaxpr/ppermute | solution.py:16
  237.1 5.3 %collective-permute-done = bf16[256,256]{1,0:T(8,128)(2,1)S(1)} collective-permute-done((bf16[256,256]{1,0:T(8,128)(2,1)S(1)}, bf16[256,256]{1,0:T(8,128)(2,1)S(1)}, u32[]{:S(2)}, u32[]{:S(2)}) %collective-permute-start) | collective-permute-done | bytes 131104 | tf_op jit(solution)/shard_map/while/body/eval_jaxpr/ppermute | solution.py:16
  243.9 5.3 %collective-permute-done = bf16[256,256]{1,0:T(8,128)(2,1)S(1)} collective-permute-done((bf16[256,256]{1,0:T(8,128)(2,1)S(1)}, bf16[256,256]{1,0:T(8,128)(2,1)S(1)}, u32[]{:S(2)}, u32[]{:S(2)}) %collective-permute-start) | collective-permute-done | bytes 131104 | tf_op jit(solution)/shard_map/while/body/eval_jaxpr/ppermute | solution.py:16
  250.6 5.3 %collective-permute-done = bf16[256,256]{1,0:T(8,128)(2,1)S(1)} collective-permute-done((bf16[256,256]{1,0:T(8,128)(2,1)S(1)}, bf16[256,256]{1,0:T(8,128)(2,1)S(1)}, u32[]{:S(2)}, u32[]{:S(2)}) %collective-permute-start) | collective-permute-done | bytes 131104 | tf_op jit(solution)/shard_map/while/body/eval_jaxpr/ppermute | solution.py:16
  257.3 5.3 %collective-permute-done = bf16[256,256]{1,0:T(8,128)(2,1)S(1)} collective-permute-done((bf16[256,256]{1,0:T(8,128)(2,1)S(1)}, bf16[256,256]{1,0:T(8,128)(2,1)S(1)}, u32[]{:S(2)}, u32[]{:S(2)}) %collective-permute-start) | collective-permute-done | bytes 131104 | tf_op jit(solution)/shard_map/while/body/eval_jaxpr/ppermute | solution.py:16
  (425 shorter events, 70.1 us)
Async XLA Ops:
  6.5 46.8 %all-gather.2.cloned.1.call-start = ((), (), s32[]{:S(2)}) async-start(), calls=%async_computation.1 | async-start | bytes 2621440 | tf_op jit(solution)/shard_map/all_gather | solution.py:50
  11.4 38.8 %all-to-all-start = ((bf16[32,8,512]{2,1,0:T(8,128)(2,1)}), bf16[32,8,512]{2,1,0:T(8,128)(2,1)S(1)}, u32[]{:S(2)}, u32[]{:S(2)}) async-start(bf16[32,8,512]{2,1,0:T(8,128)(2,1)} %broadcast_select_fusion), calls=%async_computation | async-start | bytes 524288 | tf_op jit(solution)/shard_map/all_to_all | solution.py:102
  63.2 4.4 %collective-permute-start = (bf16[256,256]{1,0:T(8,128)(2,1)S(1)}, bf16[256,256]{1,0:T(8,128)(2,1)S(1)}, u32[]{:S(2)}, u32[]{:S(2)}) collective-permute-start(bf16[256,256]{1,0:T(8,128)(2,1)S(1)} %get-tuple-element.418), channel_id=1, source_target_pairs={{124,0},{0,4},{4,8},{8,12},{12,16},{16,20},{20,24},{24,28},{28,32}... | collective-permute-start | bytes 393224 | tf_op jit(solution)/shard_map/while/body/eval_jaxpr/ppermute | solution.py:16
  68.8 5.1 %collective-permute-start = (bf16[256,256]{1,0:T(8,128)(2,1)S(1)}, bf16[256,256]{1,0:T(8,128)(2,1)S(1)}, u32[]{:S(2)}, u32[]{:S(2)}) collective-permute-start(bf16[256,256]{1,0:T(8,128)(2,1)S(1)} %get-tuple-element.418), channel_id=1, source_target_pairs={{124,0},{0,4},{4,8},{8,12},{12,16},{16,20},{20,24},{24,28},{28,32}... | collective-permute-start | bytes 393224 | tf_op jit(solution)/shard_map/while/body/eval_jaxpr/ppermute | solution.py:16
  75.0 5.6 %collective-permute-start = (bf16[256,256]{1,0:T(8,128)(2,1)S(1)}, bf16[256,256]{1,0:T(8,128)(2,1)S(1)}, u32[]{:S(2)}, u32[]{:S(2)}) collective-permute-start(bf16[256,256]{1,0:T(8,128)(2,1)S(1)} %get-tuple-element.418), channel_id=1, source_target_pairs={{124,0},{0,4},{4,8},{8,12},{12,16},{16,20},{20,24},{24,28},{28,32}... | collective-permute-start | bytes 393224 | tf_op jit(solution)/shard_map/while/body/eval_jaxpr/ppermute | solution.py:16
  81.7 5.6 %collective-permute-start = (bf16[256,256]{1,0:T(8,128)(2,1)S(1)}, bf16[256,256]{1,0:T(8,128)(2,1)S(1)}, u32[]{:S(2)}, u32[]{:S(2)}) collective-permute-start(bf16[256,256]{1,0:T(8,128)(2,1)S(1)} %get-tuple-element.418), channel_id=1, source_target_pairs={{124,0},{0,4},{4,8},{8,12},{12,16},{16,20},{20,24},{24,28},{28,32}... | collective-permute-start | bytes 393224 | tf_op jit(solution)/shard_map/while/body/eval_jaxpr/ppermute | solution.py:16
  88.5 5.6 %collective-permute-start = (bf16[256,256]{1,0:T(8,128)(2,1)S(1)}, bf16[256,256]{1,0:T(8,128)(2,1)S(1)}, u32[]{:S(2)}, u32[]{:S(2)}) collective-permute-start(bf16[256,256]{1,0:T(8,128)(2,1)S(1)} %get-tuple-element.418), channel_id=1, source_target_pairs={{124,0},{0,4},{4,8},{8,12},{12,16},{16,20},{20,24},{24,28},{28,32}... | collective-permute-start | bytes 393224 | tf_op jit(solution)/shard_map/while/body/eval_jaxpr/ppermute | solution.py:16
  95.2 5.6 %collective-permute-start = (bf16[256,256]{1,0:T(8,128)(2,1)S(1)}, bf16[256,256]{1,0:T(8,128)(2,1)S(1)}, u32[]{:S(2)}, u32[]{:S(2)}) collective-permute-start(bf16[256,256]{1,0:T(8,128)(2,1)S(1)} %get-tuple-element.418), channel_id=1, source_target_pairs={{124,0},{0,4},{4,8},{8,12},{12,16},{16,20},{20,24},{24,28},{28,32}... | collective-permute-start | bytes 393224 | tf_op jit(solution)/shard_map/while/body/eval_jaxpr/ppermute | solution.py:16
  101.9 5.6 %collective-permute-start = (bf16[256,256]{1,0:T(8,128)(2,1)S(1)}, bf16[256,256]{1,0:T(8,128)(2,1)S(1)}, u32[]{:S(2)}, u32[]{:S(2)}) collective-permute-start(bf16[256,256]{1,0:T(8,128)(2,1)S(1)} %get-tuple-element.418), channel_id=1, source_target_pairs={{124,0},{0,4},{4,8},{8,12},{12,16},{16,20},{20,24},{24,28},{28,32}... | collective-permute-start | bytes 393224 | tf_op jit(solution)/shard_map/while/body/eval_jaxpr/ppermute | solution.py:16
  108.7 5.6 %collective-permute-start = (bf16[256,256]{1,0:T(8,128)(2,1)S(1)}, bf16[256,256]{1,0:T(8,128)(2,1)S(1)}, u32[]{:S(2)}, u32[]{:S(2)}) collective-permute-start(bf16[256,256]{1,0:T(8,128)(2,1)S(1)} %get-tuple-element.418), channel_id=1, source_target_pairs={{124,0},{0,4},{4,8},{8,12},{12,16},{16,20},{20,24},{24,28},{28,32}... | collective-permute-start | bytes 393224 | tf_op jit(solution)/shard_map/while/body/eval_jaxpr/ppermute | solution.py:16
  115.4 5.6 %collective-permute-start = (bf16[256,256]{1,0:T(8,128)(2,1)S(1)}, bf16[256,256]{1,0:T(8,128)(2,1)S(1)}, u32[]{:S(2)}, u32[]{:S(2)}) collective-permute-start(bf16[256,256]{1,0:T(8,128)(2,1)S(1)} %get-tuple-element.418), channel_id=1, source_target_pairs={{124,0},{0,4},{4,8},{8,12},{12,16},{16,20},{20,24},{24,28},{28,32}... | collective-permute-start | bytes 393224 | tf_op jit(solution)/shard_map/while/body/eval_jaxpr/ppermute | solution.py:16
  122.2 5.6 %collective-permute-start = (bf16[256,256]{1,0:T(8,128)(2,1)S(1)}, bf16[256,256]{1,0:T(8,128)(2,1)S(1)}, u32[]{:S(2)}, u32[]{:S(2)}) collective-permute-start(bf16[256,256]{1,0:T(8,128)(2,1)S(1)} %get-tuple-element.418), channel_id=1, source_target_pairs={{124,0},{0,4},{4,8},{8,12},{12,16},{16,20},{20,24},{24,28},{28,32}... | collective-permute-start | bytes 393224 | tf_op jit(solution)/shard_map/while/body/eval_jaxpr/ppermute | solution.py:16
  128.9 5.6 %collective-permute-start = (bf16[256,256]{1,0:T(8,128)(2,1)S(1)}, bf16[256,256]{1,0:T(8,128)(2,1)S(1)}, u32[]{:S(2)}, u32[]{:S(2)}) collective-permute-start(bf16[256,256]{1,0:T(8,128)(2,1)S(1)} %get-tuple-element.418), channel_id=1, source_target_pairs={{124,0},{0,4},{4,8},{8,12},{12,16},{16,20},{20,24},{24,28},{28,32}... | collective-permute-start | bytes 393224 | tf_op jit(solution)/shard_map/while/body/eval_jaxpr/ppermute | solution.py:16
  135.7 5.6 %collective-permute-start = (bf16[256,256]{1,0:T(8,128)(2,1)S(1)}, bf16[256,256]{1,0:T(8,128)(2,1)S(1)}, u32[]{:S(2)}, u32[]{:S(2)}) collective-permute-start(bf16[256,256]{1,0:T(8,128)(2,1)S(1)} %get-tuple-element.418), channel_id=1, source_target_pairs={{124,0},{0,4},{4,8},{8,12},{12,16},{16,20},{20,24},{24,28},{28,32}... | collective-permute-start | bytes 393224 | tf_op jit(solution)/shard_map/while/body/eval_jaxpr/ppermute | solution.py:16
  142.4 5.6 %collective-permute-start = (bf16[256,256]{1,0:T(8,128)(2,1)S(1)}, bf16[256,256]{1,0:T(8,128)(2,1)S(1)}, u32[]{:S(2)}, u32[]{:S(2)}) collective-permute-start(bf16[256,256]{1,0:T(8,128)(2,1)S(1)} %get-tuple-element.418), channel_id=1, source_target_pairs={{124,0},{0,4},{4,8},{8,12},{12,16},{16,20},{20,24},{24,28},{28,32}... | collective-permute-start | bytes 393224 | tf_op jit(solution)/shard_map/while/body/eval_jaxpr/ppermute | solution.py:16
  149.1 5.6 %collective-permute-start = (bf16[256,256]{1,0:T(8,128)(2,1)S(1)}, bf16[256,256]{1,0:T(8,128)(2,1)S(1)}, u32[]{:S(2)}, u32[]{:S(2)}) collective-permute-start(bf16[256,256]{1,0:T(8,128)(2,1)S(1)} %get-tuple-element.418), channel_id=1, source_target_pairs={{124,0},{0,4},{4,8},{8,12},{12,16},{16,20},{20,24},{24,28},{28,32}... | collective-permute-start | bytes 393224 | tf_op jit(solution)/shard_map/while/body/eval_jaxpr/ppermute | solution.py:16
  155.9 5.6 %collective-permute-start = (bf16[256,256]{1,0:T(8,128)(2,1)S(1)}, bf16[256,256]{1,0:T(8,128)(2,1)S(1)}, u32[]{:S(2)}, u32[]{:S(2)}) collective-permute-start(bf16[256,256]{1,0:T(8,128)(2,1)S(1)} %get-tuple-element.418), channel_id=1, source_target_pairs={{124,0},{0,4},{4,8},{8,12},{12,16},{16,20},{20,24},{24,28},{28,32}... | collective-permute-start | bytes 393224 | tf_op jit(solution)/shard_map/while/body/eval_jaxpr/ppermute | solution.py:16
  162.6 5.6 %collective-permute-start = (bf16[256,256]{1,0:T(8,128)(2,1)S(1)}, bf16[256,256]{1,0:T(8,128)(2,1)S(1)}, u32[]{:S(2)}, u32[]{:S(2)}) collective-permute-start(bf16[256,256]{1,0:T(8,128)(2,1)S(1)} %get-tuple-element.418), channel_id=1, source_target_pairs={{124,0},{0,4},{4,8},{8,12},{12,16},{16,20},{20,24},{24,28},{28,32}... | collective-permute-start | bytes 393224 | tf_op jit(solution)/shard_map/while/body/eval_jaxpr/ppermute | solution.py:16
  169.4 5.6 %collective-permute-start = (bf16[256,256]{1,0:T(8,128)(2,1)S(1)}, bf16[256,256]{1,0:T(8,128)(2,1)S(1)}, u32[]{:S(2)}, u32[]{:S(2)}) collective-permute-start(bf16[256,256]{1,0:T(8,128)(2,1)S(1)} %get-tuple-element.418), channel_id=1, source_target_pairs={{124,0},{0,4},{4,8},{8,12},{12,16},{16,20},{20,24},{24,28},{28,32}... | collective-permute-start | bytes 393224 | tf_op jit(solution)/shard_map/while/body/eval_jaxpr/ppermute | solution.py:16
  176.1 5.6 %collective-permute-start = (bf16[256,256]{1,0:T(8,128)(2,1)S(1)}, bf16[256,256]{1,0:T(8,128)(2,1)S(1)}, u32[]{:S(2)}, u32[]{:S(2)}) collective-permute-start(bf16[256,256]{1,0:T(8,128)(2,1)S(1)} %get-tuple-element.418), channel_id=1, source_target_pairs={{124,0},{0,4},{4,8},{8,12},{12,16},{16,20},{20,24},{24,28},{28,32}... | collective-permute-start | bytes 393224 | tf_op jit(solution)/shard_map/while/body/eval_jaxpr/ppermute | solution.py:16
  182.8 5.6 %collective-permute-start = (bf16[256,256]{1,0:T(8,128)(2,1)S(1)}, bf16[256,256]{1,0:T(8,128)(2,1)S(1)}, u32[]{:S(2)}, u32[]{:S(2)}) collective-permute-start(bf16[256,256]{1,0:T(8,128)(2,1)S(1)} %get-tuple-element.418), channel_id=1, source_target_pairs={{124,0},{0,4},{4,8},{8,12},{12,16},{16,20},{20,24},{24,28},{28,32}... | collective-permute-start | bytes 393224 | tf_op jit(solution)/shard_map/while/body/eval_jaxpr/ppermute | solution.py:16
  189.6 5.6 %collective-permute-start = (bf16[256,256]{1,0:T(8,128)(2,1)S(1)}, bf16[256,256]{1,0:T(8,128)(2,1)S(1)}, u32[]{:S(2)}, u32[]{:S(2)}) collective-permute-start(bf16[256,256]{1,0:T(8,128)(2,1)S(1)} %get-tuple-element.418), channel_id=1, source_target_pairs={{124,0},{0,4},{4,8},{8,12},{12,16},{16,20},{20,24},{24,28},{28,32}... | collective-permute-start | bytes 393224 | tf_op jit(solution)/shard_map/while/body/eval_jaxpr/ppermute | solution.py:16
  196.3 5.6 %collective-permute-start = (bf16[256,256]{1,0:T(8,128)(2,1)S(1)}, bf16[256,256]{1,0:T(8,128)(2,1)S(1)}, u32[]{:S(2)}, u32[]{:S(2)}) collective-permute-start(bf16[256,256]{1,0:T(8,128)(2,1)S(1)} %get-tuple-element.418), channel_id=1, source_target_pairs={{124,0},{0,4},{4,8},{8,12},{12,16},{16,20},{20,24},{24,28},{28,32}... | collective-permute-start | bytes 393224 | tf_op jit(solution)/shard_map/while/body/eval_jaxpr/ppermute | solution.py:16
  203.1 5.6 %collective-permute-start = (bf16[256,256]{1,0:T(8,128)(2,1)S(1)}, bf16[256,256]{1,0:T(8,128)(2,1)S(1)}, u32[]{:S(2)}, u32[]{:S(2)}) collective-permute-start(bf16[256,256]{1,0:T(8,128)(2,1)S(1)} %get-tuple-element.418), channel_id=1, source_target_pairs={{124,0},{0,4},{4,8},{8,12},{12,16},{16,20},{20,24},{24,28},{28,32}... | collective-permute-start | bytes 393224 | tf_op jit(solution)/shard_map/while/body/eval_jaxpr/ppermute | solution.py:16
  209.8 5.6 %collective-permute-start = (bf16[256,256]{1,0:T(8,128)(2,1)S(1)}, bf16[256,256]{1,0:T(8,128)(2,1)S(1)}, u32[]{:S(2)}, u32[]{:S(2)}) collective-permute-start(bf16[256,256]{1,0:T(8,128)(2,1)S(1)} %get-tuple-element.418), channel_id=1, source_target_pairs={{124,0},{0,4},{4,8},{8,12},{12,16},{16,20},{20,24},{24,28},{28,32}... | collective-permute-start | bytes 393224 | tf_op jit(solution)/shard_map/while/body/eval_jaxpr/ppermute | solution.py:16
  216.6 5.6 %collective-permute-start = (bf16[256,256]{1,0:T(8,128)(2,1)S(1)}, bf16[256,256]{1,0:T(8,128)(2,1)S(1)}, u32[]{:S(2)}, u32[]{:S(2)}) collective-permute-start(bf16[256,256]{1,0:T(8,128)(2,1)S(1)} %get-tuple-element.418), channel_id=1, source_target_pairs={{124,0},{0,4},{4,8},{8,12},{12,16},{16,20},{20,24},{24,28},{28,32}... | collective-permute-start | bytes 393224 | tf_op jit(solution)/shard_map/while/body/eval_jaxpr/ppermute | solution.py:16
  223.3 5.6 %collective-permute-start = (bf16[256,256]{1,0:T(8,128)(2,1)S(1)}, bf16[256,256]{1,0:T(8,128)(2,1)S(1)}, u32[]{:S(2)}, u32[]{:S(2)}) collective-permute-start(bf16[256,256]{1,0:T(8,128)(2,1)S(1)} %get-tuple-element.418), channel_id=1, source_target_pairs={{124,0},{0,4},{4,8},{8,12},{12,16},{16,20},{20,24},{24,28},{28,32}... | collective-permute-start | bytes 393224 | tf_op jit(solution)/shard_map/while/body/eval_jaxpr/ppermute | solution.py:16
  230.0 5.6 %collective-permute-start = (bf16[256,256]{1,0:T(8,128)(2,1)S(1)}, bf16[256,256]{1,0:T(8,128)(2,1)S(1)}, u32[]{:S(2)}, u32[]{:S(2)}) collective-permute-start(bf16[256,256]{1,0:T(8,128)(2,1)S(1)} %get-tuple-element.418), channel_id=1, source_target_pairs={{124,0},{0,4},{4,8},{8,12},{12,16},{16,20},{20,24},{24,28},{28,32}... | collective-permute-start | bytes 393224 | tf_op jit(solution)/shard_map/while/body/eval_jaxpr/ppermute | solution.py:16
  236.8 5.6 %collective-permute-start = (bf16[256,256]{1,0:T(8,128)(2,1)S(1)}, bf16[256,256]{1,0:T(8,128)(2,1)S(1)}, u32[]{:S(2)}, u32[]{:S(2)}) collective-permute-start(bf16[256,256]{1,0:T(8,128)(2,1)S(1)} %get-tuple-element.418), channel_id=1, source_target_pairs={{124,0},{0,4},{4,8},{8,12},{12,16},{16,20},{20,24},{24,28},{28,32}... | collective-permute-start | bytes 393224 | tf_op jit(solution)/shard_map/while/body/eval_jaxpr/ppermute | solution.py:16
  243.5 5.6 %collective-permute-start = (bf16[256,256]{1,0:T(8,128)(2,1)S(1)}, bf16[256,256]{1,0:T(8,128)(2,1)S(1)}, u32[]{:S(2)}, u32[]{:S(2)}) collective-permute-start(bf16[256,256]{1,0:T(8,128)(2,1)S(1)} %get-tuple-element.418), channel_id=1, source_target_pairs={{124,0},{0,4},{4,8},{8,12},{12,16},{16,20},{20,24},{24,28},{28,32}... | collective-permute-start | bytes 393224 | tf_op jit(solution)/shard_map/while/body/eval_jaxpr/ppermute | solution.py:16
  250.3 5.6 %collective-permute-start = (bf16[256,256]{1,0:T(8,128)(2,1)S(1)}, bf16[256,256]{1,0:T(8,128)(2,1)S(1)}, u32[]{:S(2)}, u32[]{:S(2)}) collective-permute-start(bf16[256,256]{1,0:T(8,128)(2,1)S(1)} %get-tuple-element.418), channel_id=1, source_target_pairs={{124,0},{0,4},{4,8},{8,12},{12,16},{16,20},{20,24},{24,28},{28,32}... | collective-permute-start | bytes 393224 | tf_op jit(solution)/shard_map/while/body/eval_jaxpr/ppermute | solution.py:16
  257.0 5.6 %collective-permute-start = (bf16[256,256]{1,0:T(8,128)(2,1)S(1)}, bf16[256,256]{1,0:T(8,128)(2,1)S(1)}, u32[]{:S(2)}, u32[]{:S(2)}) collective-permute-start(bf16[256,256]{1,0:T(8,128)(2,1)S(1)} %get-tuple-element.418), channel_id=1, source_target_pairs={{124,0},{0,4},{4,8},{8,12},{12,16},{16,20},{20,24},{24,28},{28,32}... | collective-permute-start | bytes 393224 | tf_op jit(solution)/shard_map/while/body/eval_jaxpr/ppermute | solution.py:16
  (5 other events, 81.3 us)
Sparse Core Ops, SparseCore 0:
  9.5 43.8 all-gather.1
where the time goes:
time: 275 us; the launch traced here: 272 us
  waiting for transfers between devices  175 us (64%)
  matrix products  29.8 us (11%)
  starting transfers between devices  26.3 us (10%)
  other arithmetic  18.6 us (7%)
  between operations  13.6 us (5%)
  local copies, waits for them, and re-layouts  5.73 us (2%)
  loops' own time  2.97 us (1%)
    ppermute x31, waiting for transfers between devices, from_behind(): return lax.ppermute(block, axis, route)  151 us
    all_to_all x1, waiting for transfers between devices, local(): lax.all_to_all(jnp.take(shaped, mine, axis=0).reshape(rows, query.shape[1...  19.9 us
    all_to_all x1, starting transfers between devices, local(): lax.all_to_all(jnp.take(shaped, mine, axis=0).reshape(rows, query.shape[1...  16.7 us
    dot_general x32, matrix products, attend(): jnp.einsum('cgqk,kcd->cgqd', weights.astype(jnp.bfloat16), vhead, preferr...  16 us
    dot_general x32, matrix products, attend(): jnp.einsum('qcgd,kcd->cgqk', qheads, khead, preferred_element_type=jnp.fl...  10.4 us
    ppermute x31, starting transfers between devices, from_behind(): return lax.ppermute(block, axis, route)  9.58 us
    reduce_sum x32, other arithmetic, attend(): total = total * keep + jnp.sum(weights, axis=-1)  6.65 us
  transfers between devices with their start and end apart: 33, of which 33 were waited for; matrix products, arithmetic and copies ran while one was open for 5% of the time, Pallas kernels for 0%

commit v1 on v0

v1 whole, which is shorter than its diff:
```python
import functools

import jax
import jax.numpy as jnp
import numpy as np
from jax import lax
from jax.experimental import pallas as pl
from jax.experimental.pallas import tpu as pltpu
from jax.sharding import PartitionSpec as P

HD = 128
GROUP = 4
ROWS = 256
BROW = 8
NCTX = 32
NHEAD = 4
NDOCS = 16
FEAT = 1024
BEHIND = 8
ROPE_BASE = 500000.0
MASKED = -1e30
MESH = pl.DeviceIdType.MESH

SHIFT = 2
CHUNKS = 8
DEPTH = 3

R = ROWS // CHUNKS
BACKWARD = SHIFT
FORWARD = BEHIND // 2 - SHIFT
HOPS = max(FORWARD, BACKWARD)
LAG = 2 + (HOPS - 1) // 2
OWN = BEHIND - 2 * SHIFT
QROWS = GROUP * ROWS
RB = 128
BLOCK = GROUP * BROW
EXPC = float(np.log2(np.e) / np.sqrt(HD))

F32 = jnp.float32
BF16 = jnp.bfloat16


def when(cond):
    if isinstance(cond, (bool, np.bool_)):
        return (lambda f: f()) if cond else (lambda f: None)
    return pl.when(cond)


def both(*conds):
    out = True
    for c in conds:
        if isinstance(c, (bool, np.bool_)):
            if not c:
                return False
        else:
            out = c if out is True else jnp.logical_and(out, c)
    return out


def kernel(
    tokens, query, w_key, w_value, lengths, balance, freq, out,
    gath, wkv, part, cosf, sinf, kv, kvd, qbuf, q2, qidx, mx, tot, acc, stage, recv,
    local_sem, tsend, trecv, zsend, zrecv, ssend, srecv, qsend, qrecv, osend, orecv,
):
    x = lax.axis_index("dp")
    me = lax.axis_index("ctx")
    y = lax.axis_index("head")
    z = me // 2
    core = lax.rem(me, 2)
    up = lax.rem(y + 1, NHEAD)
    down = lax.rem(y + NHEAD - 1, NHEAD)
    opposite = lax.rem(y + 2, NHEAD)
    ahead = lax.rem(me + 2, NCTX)
    behind = lax.rem(me + NCTX - 2, NCTX)
    sibling = me + 1 - 2 * core
    qshard = lax.rem(me + 2 * SHIFT, NCTX)

    def remote(src, dst, ssem, rsem, ctx, head):
        return pltpu.make_async_remote_copy(
            src_ref=src, dst_ref=dst, send_sem=ssem, recv_sem=rsem,
            device_id=(x, ctx, head), device_id_type=MESH,
        )

    def own_copy(c, p):
        rows = pl.ds(c * R, R)
        return remote(
            tokens.at[rows, :], gath.at[1 + p, rows, :], tsend.at[p, c], trecv.at[p, c],
            me, up if p == 0 else down,
        )

    def relay_copy(c, p):
        rows = pl.ds(c * R + p * (R // 2), R // 2)
        return remote(
            gath.at[1 + p, rows, :], gath.at[3, rows, :], tsend.at[2 + p, c], trecv.at[2 + p, c],
            me, up if p == 0 else down,
        )

    def slot(c, u):
        if u == BEHIND:
            return kvd.at[pl.ds(c * R, R), pl.ds(0, 2 * HD)]
        return kv.at[c, pl.ds(u * R, R), pl.ds(0, 2 * HD)]

    def hop_copy(c, sign, h):
        index = h - 1 if sign > 0 else FORWARD + h - 1
        return remote(
            slot(c, OWN - sign * 2 * (h - 1)), slot(c, OWN - sign * 2 * h),
            zsend.at[index, c], zrecv.at[index, c], ahead if sign > 0 else behind, y,
        )

    def sib_copy(c, u):
        there = pl.multiple_of((u - 1 + 2 * core) * R, R)
        return remote(
            slot(c, u), kv.at[c, pl.ds(there, R), pl.ds(0, 2 * HD)],
            ssend.at[u // 2, c], srecv.at[u // 2 - 1 + core, c], sibling, y,
        )

    def sib_cond(u):
        if u == 0:
            return core == 1
        if u == BEHIND:
            return core == 0
        return True

    def sib_start(c, u):
        @when(sib_cond(u))
        def _():
            sib_copy(c, u).start()

    def sib_wait(c, k):
        remote(
            slot(c, 2 * k), slot(c, 2 * k + 1), ssend.at[k, c], srecv.at[k, c], sibling, y
        ).wait_recv()

    query_copy = remote(
        query, qbuf, qsend.at[0], qrecv.at[0], lax.rem(me + NCTX - 2 * SHIFT, NCTX), y
    )

    barrier = pltpu.get_barrier_semaphore()

    def greet(o, carry):
        pl.semaphore_signal(
            barrier, inc=1, device_id=(x, lax.rem(me + o, NCTX), y), device_id_type=MESH
        )
        return carry

    for head in (up, down):
        pl.semaphore_signal(barrier, inc=1, device_id=(x, me, head), device_id_type=MESH)
    lax.fori_loop(1, NCTX, greet, 0)

    loads = [
        pltpu.make_async_copy(tokens, gath.at[0], local_sem.at[0]),
        pltpu.make_async_copy(w_value, wkv.at[:, pl.ds(0, HD)], local_sem.at[1]),
        pltpu.make_async_copy(w_key, wkv.at[:, pl.ds(HD, HD)], local_sem.at[2]),
    ]
    if SHIFT == 0:
        loads.append(pltpu.make_async_copy(query, qbuf, local_sem.at[3]))
    for load in loads:
        load.start()

    pl.semaphore_wait(barrier, NCTX - 1 + 2)

    for c in range(DEPTH):
        for p in range(2):
            own_copy(c, p).start()
    if SHIFT:
        query_copy.start()

    lane = lax.broadcasted_iota(jnp.int32, (1, HD), 1)
    low = jnp.zeros((1, HD), jnp.int32)
    high = jnp.zeros((1, HD), jnp.int32)
    edge = jnp.int32(0)
    for j in range(NDOCS):
        low = jnp.where(lane == j, edge, low)
        edge = edge + lengths[j]
        high = jnp.where(lane == j, edge, high)

    def in_doc(pos):
        return (pos >= low) & (pos < high)

    pos = me * ROWS + lax.broadcasted_iota(jnp.int32, (ROWS, HD), 0)
    angle = pos.astype(F32) * freq[...]
    cosf[...] = jnp.cos(angle)
    sine = jnp.sin(angle)
    sinf[...] = jnp.where(lax.broadcasted_iota(jnp.int32, (ROWS, HD), 1) < HD // 2, -sine, sine)

    def mark(c, carry):
        row = lax.broadcasted_iota(jnp.int32, (BEHIND * R, HD), 0)
        shard = (me + NCTX - BEHIND + 2 * SHIFT + row // R) & (NCTX - 1)
        kpos = shard * ROWS + c * R + (row & (R - 1))
        kv[c, :, pl.ds(2 * HD, HD)] = jnp.where(in_doc(kpos), 0.0, MASKED).astype(BF16)
        return carry

    lax.fori_loop(0, CHUNKS, mark, 0)
    qpos = qshard * ROWS + lax.broadcasted_iota(jnp.int32, (ROWS, HD), 0)
    kvd[:, pl.ds(2 * HD, HD)] = jnp.where(in_doc(qpos), 0.0, MASKED).astype(BF16)

    mx[...] = jnp.full_like(mx, MASKED)
    tot[...] = jnp.zeros_like(tot)
    acc[...] = jnp.zeros_like(acc)
    for load in loads:
        load.wait()

    def dest_of(n, e):
        if isinstance(n, int):
            dz = 8 - n if e < 2 else (0 if n == 0 else n - 8)
        else:
            dz = 8 - n if e < 2 else jnp.where(n == 0, 0, n - 8)
        return ((z + 16 + dz) & 15) * 2 + ((core + e) & 1)

    def prepare_query():
        if SHIFT:
            query_copy.wait_recv()
        r = lax.broadcasted_iota(jnp.int32, (ROWS, NCTX), 0)
        n = r >> 5
        e = (r >> 3) & 3
        dz = jnp.where(e < 2, 8 - n, jnp.where(n == 0, 0, n - 8))
        dest = ((z + 16 + dz) & 15) * 2 + ((core + e) & 1)
        bal = balance[pl.ds(qshard, 1), :]
        pick = jnp.where(bal == dest, 1.0, 0.0).astype(BF16)
        b = lax.broadcasted_iota(jnp.int32, (NCTX, ROWS), 0)
        c = lax.broadcasted_iota(jnp.int32, (NCTX, ROWS), 1)
        widen = jnp.where((c >> 3) == b, 1.0, 0.0).astype(BF16)
        spread = jnp.dot(pick, widen, preferred_element_type=F32)
        r = lax.broadcasted_iota(jnp.int32, (ROWS, ROWS), 0)
        c = lax.broadcasted_iota(jnp.int32, (ROWS, ROWS), 1)
        perm = jnp.where((c & 7) == (r & 7), spread, 0.0).astype(BF16)
        moved = jnp.dot(perm, qbuf[...], preferred_element_type=F32)
        doc = jnp.where(in_doc(qpos), 1.0, 0.0).astype(BF16)
        doc = jnp.dot(perm, doc, preferred_element_type=F32)
        index = lax.broadcasted_iota(jnp.int32, (ROWS, HD), 0).astype(F32).astype(BF16)
        index = jnp.dot(perm, index, preferred_element_type=F32)

        def rows_of(parts):
            parts = [p.reshape(NCTX, BROW, HD) for p in parts]
            return jnp.stack(parts, axis=1).reshape(QROWS, HD)

        q2[:, pl.ds(0, HD)] = rows_of(
            [moved[:, g * HD : (g + 1) * HD] for g in range(GROUP)]
        ).astype(BF16)
        q2[:, pl.ds(HD, HD)] = rows_of([doc] * GROUP).astype(BF16)
        qidx[...] = rows_of([index] * GROUP)

    def nt(a, b):
        return lax.dot_general(a, b, (((1,), (1,)), ((), ())), preferred_element_type=F32)

    def update(rows, score, values):
        width = score.shape[1]
        old = mx[rows, :]
        new = jnp.maximum(old, jnp.max(score, axis=1, keepdims=True))
        keep = jnp.exp2((old - new) * EXPC)
        wide = jnp.concatenate([new] * (width // HD), axis=1) if width > HD else new
        weight = jnp.exp2((score - wide) * EXPC)
        lanes = weight[:, :HD]
        for k in range(1, width // HD):
            lanes = lanes + weight[:, k * HD : (k + 1) * HD]
        mx[rows, :] = new
        tot[rows, :] = tot[rows, :] * keep + lanes
        acc[rows, :] = acc[rows, :] * keep + jnp.dot(
            weight.astype(BF16), values, preferred_element_type=F32
        )

    def plain(c, rows):
        score = nt(q2[rows, :], kv[c, :, pl.ds(HD, 2 * HD)])
        update(rows, score, kv[c, :, pl.ds(0, HD)])

    def diagonal(half, rows):
        keys = pl.ds(half * HD, HD)
        score = nt(q2[rows, :], kvd[keys, pl.ds(HD, 2 * HD)])
        kidx = (half * HD + lax.broadcasted_iota(jnp.int32, (RB, HD), 1)).astype(F32)
        score = jnp.where(kidx <= qidx[rows, :], score, MASKED)
        update(rows, score, kvd[keys, pl.ds(0, HD)])

    def out_copy(n, e):
        rows = pl.ds(pl.multiple_of((n * 4 + e) * BLOCK, BLOCK), BLOCK)
        there = pl.ds(pl.multiple_of(qshard * BLOCK, BLOCK), BLOCK)
        return remote(
            stage.at[rows, :], recv.at[there, :], osend.at[n * 4 + e], orecv.at[qshard],
            dest_of(n, e), y,
        )

    def hops(c, h):
        if h <= FORWARD:
            hop_copy(c, 1, h).wait_recv()
            if h < FORWARD:
                hop_copy(c, 1, h + 1).start()
            sib_start(c, OWN - 2 * h)
        if h <= BACKWARD:
            hop_copy(c, -1, h).wait_recv()
            if h < BACKWARD:
                hop_copy(c, -1, h + 1).start()
            sib_start(c, OWN + 2 * h)

    def iteration(i, last):
        @when(i < CHUNKS)
        def _():
            for p in range(2):
                own_copy(i, p).wait_recv()
                relay_copy(i, p).start()

        @when(i + DEPTH < CHUNKS)
        def _():
            for p in range(2):
                own_copy(i + DEPTH, p).start()

        for h in range(1, HOPS + 1, 2):
            c = i - 2 - h // 2

            @when(both(c >= 0, c < CHUNKS))
            def _():
                hops(c, h)

        @when(i < CHUNKS)
        def _():
            rows = pl.ds(i * R, R)
            total = None
            for s, source in enumerate((y, down, up)):
                term = jnp.dot(
                    gath[s, rows, :], wkv[pl.ds(pl.multiple_of(source * FEAT, FEAT), FEAT), :],
                    preferred_element_type=F32,
                )
                total = term if total is None else total + term
            part[rows, :] = total

        @when(both(i >= 1, i <= CHUNKS))
        def _():
            c = i - 1
            rows = pl.ds(c * R, R)
            for p in range(2):
                relay_copy(c, p).wait_recv()
            raw = part[rows, :] + jnp.dot(
                gath[3, rows, :], wkv[pl.ds(pl.multiple_of(opposite * FEAT, FEAT), FEAT), :],
                preferred_element_type=F32,
            )
            value = raw[:, :HD]
            key = raw[:, HD:]
            key = key * cosf[rows, :] + pltpu.roll(key, HD // 2, 1) * sinf[rows, :]
            slot(c, OWN)[...] = jnp.concatenate([value, key], axis=1).astype(BF16)
            if FORWARD:
                hop_copy(c, 1, 1).start()
            if BACKWARD:
                hop_copy(c, -1, 1).start()
            sib_start(c, OWN)

        for h in range(2, HOPS + 1, 2):
            c = i - 2 - (h - 1) // 2

            @when(both(c >= 0, c < CHUNKS))
            def _():
                hops(c, h)

        a = i - LAG
        if last:
            for k in range(4):
                sib_wait(a, k)
        else:
            @when(i == LAG)
            def _():
                prepare_query()

            @when(a >= 0)
            def _():
                for k in range(4):
                    sib_wait(a, k)

                def block(rb, carry):
                    plain(a, pl.ds(pl.multiple_of(rb * RB, RB), RB))
                    return carry

                lax.fori_loop(0, QROWS // RB, block, 0)

            @when(a == CHUNKS // 2 - 1)
            def _():
                def block(rb, carry):
                    diagonal(0, pl.ds(pl.multiple_of(rb * RB, RB), RB))
                    return carry

                lax.fori_loop(0, QROWS // RB, block, 0)

    def loop_body(i, carry):
        iteration(i, False)
        return carry

    final = CHUNKS + LAG - 1
    lax.fori_loop(0, final, loop_body, 0)
    iteration(final, True)

    def finish(rb, carry):
        rows = pl.ds(pl.multiple_of(rb * RB, RB), RB)
        plain(CHUNKS - 1, rows)
        diagonal(1, rows)
        total = jnp.sum(tot[rows, :], axis=1, keepdims=True)
        stage[rows, :] = (acc[rows, :] / total).astype(BF16)
        for e in range(4):
            if e == 2:
                @pl.when(rb > 0)
                def _():
                    out_copy(rb, e).start()
            else:
                out_copy(rb, e).start()
        return carry

    lax.fori_loop(0, QROWS // RB, finish, 0)

    def arrive(dz, own):
        source = (z + 16 + dz) & 15
        chip = (source + SHIFT) & 15
        for k in range(2):
            shard = chip * 2 + k
            there = pl.ds(pl.multiple_of(shard * BLOCK, BLOCK), BLOCK)

            def landed():
                remote(
                    stage.at[pl.ds(0, BLOCK), :], recv.at[there, :], osend.at[0], orecv.at[shard],
                    sibling, y,
                ).wait_recv()

            if own:
                pl.when(core != k)(landed)
            else:
                landed()
        if own:
            there = pl.ds(pl.multiple_of(qshard * BLOCK, BLOCK), BLOCK)
            recv[there, :] = stage[pl.ds(2 * BLOCK, BLOCK), :]
        block = recv[pl.ds(pl.multiple_of(chip * 2 * BLOCK, 2 * BLOCK), 2 * BLOCK), :].astype(F32)
        heads = [
            jnp.concatenate(
                [
                    block[g * BROW : (g + 1) * BROW],
                    block[BLOCK + g * BROW : BLOCK + (g + 1) * BROW],
                ],
                axis=0,
            )
            for g in range(GROUP)
        ]
        out[pl.ds(pl.multiple_of(chip * 2 * BROW, 2 * BROW), 2 * BROW), :] = jnp.concatenate(
            heads, axis=1
        ).astype(BF16)

    arrive(0, True)
    arrive(8, False)

    def pair(n, carry):
        arrive(8 - n, False)
        arrive(n - 8, False)
        return carry

    lax.fori_loop(1, 8, pair, 0)

    def sent(c, carry):
        for p in range(2):
            own_copy(c, p).wait_send()
            relay_copy(c, p).wait_send()
        for h in range(1, FORWARD + 1):
            hop_copy(c, 1, h).wait_send()
        for h in range(1, BACKWARD + 1):
            hop_copy(c, -1, h).wait_send()
        for u in range(0, BEHIND + 1, 2):
            @when(sib_cond(u))
            def _():
                sib_copy(c, u).wait_send()
        return carry

    lax.fori_loop(0, CHUNKS, sent, 0)
    if SHIFT:
        query_copy.wait_send()

    def out_sent(n, carry):
        for e in range(4):
            if e == 2:
                @pl.when(n > 0)
                def _():
                    out_copy(n, e).wait_send()
            else:
                out_copy(n, e).wait_send()
        return carry

    lax.fori_loop(0, QROWS // RB, out_sent, 0)


def local(tokens, query, w_key, w_value, doc_lengths, balance):
    half = HD // 2
    freq = ROPE_BASE ** (-(jnp.arange(half, dtype=F32) * 2.0 / HD))
    freq = jnp.concatenate([freq, freq])[None, :]
    anywhere = pl.BlockSpec(memory_space=pl.ANY)
    vmem = pl.BlockSpec(memory_space=pltpu.VMEM)
    smem = pl.BlockSpec(memory_space=pltpu.SMEM)
    dma = pltpu.SemaphoreType.DMA
    width = 2 * HD
    return pl.pallas_call(
        kernel,
        out_shape=jax.ShapeDtypeStruct((ROWS, GROUP * HD), BF16),
        in_specs=[anywhere, anywhere, anywhere, anywhere, smem, vmem, vmem],
        out_specs=vmem,
        scratch_shapes=[
            pltpu.VMEM((NHEAD, ROWS, FEAT), BF16),
            pltpu.VMEM((NHEAD * FEAT, width), BF16),
            pltpu.VMEM((ROWS, width), F32),
            pltpu.VMEM((ROWS, HD), F32),
            pltpu.VMEM((ROWS, HD), F32),
            pltpu.VMEM((CHUNKS, BEHIND * R, 3 * HD), BF16),
            pltpu.VMEM((ROWS, 3 * HD), BF16),
            pltpu.VMEM((ROWS, GROUP * HD), BF16),
            pltpu.VMEM((QROWS, width), BF16),
            pltpu.VMEM((QROWS, HD), F32),
            pltpu.VMEM((QROWS, HD), F32),
            pltpu.VMEM((QROWS, HD), F32),
            pltpu.VMEM((QROWS, HD), F32),
            pltpu.VMEM((QROWS, HD), BF16),
            pltpu.VMEM((QROWS, HD), BF16),
            dma((4,)),
            dma((4, CHUNKS)),
            dma((4, CHUNKS)),
            dma((FORWARD + BACKWARD, CHUNKS)),
            dma((FORWARD + BACKWARD, CHUNKS)),
            dma((5, CHUNKS)),
            dma((4, CHUNKS)),
            dma((1,)),
            dma((1,)),
            dma((NCTX,)),
            dma((NCTX,)),
        ],
        compiler_params=pltpu.CompilerParams(
            collective_id=0, has_side_effects=True, vmem_limit_bytes=48 * 1024 * 1024
        ),
        name="attend",
    )(tokens, query, w_key, w_value, doc_lengths, balance, freq)


def solution(mesh):
    placed = (
        P(("dp", "ctx"), "head"),
        P(("dp", "ctx"), "head"),
        P(None, "head"),
        P(None, "head"),
        P("dp"),
        P("dp", None),
    )
    return jax.shard_map(
        local, mesh=mesh, in_specs=placed, out_specs=P(("dp", "ctx"), "head"), check_vma=False
    )
```

time: 275 us -> 111 us (0.40); the launches traced: 272 us -> 111 us
  waiting for transfers between devices: 175 us -> 0 us
  Pallas kernels: 0 us -> 104 us
  matrix products: 29.8 us -> 0 us
  starting transfers between devices: 26.3 us -> 0 us
  other arithmetic: 18.6 us -> 0.09 us
  between operations: 13.6 us -> 0.02 us
  loops' own time: 2.97 us -> 0 us
    ppermute x31 -> x0, waiting for transfers between devices: 151 us -> none  [from_behind(): return lax.ppermute(block, axis, route)]
    pallas_call x0 -> x1, Pallas kernels: none -> 104 us  [local(): pl.pallas_call(kernel, out_shape=jax.ShapeDtypeStruct((ROWS, GROUP * HD),...]
    dot_general x66 -> x0, matrix products: 29.8 us -> none  [the longest x32 16 us: attend(): jnp.einsum('cgqk,kcd->cgqd', weights.astype(jnp.bfloat16), vhead, preferr...]
    all_to_all x1 -> x0, waiting for transfers between devices: 19.9 us -> none  [local(): lax.all_to_all(jnp.take(shaped, mine, axis=0).reshape(rows, query.shape[1...]
    all_to_all x1 -> x0, starting transfers between devices: 16.7 us -> none  [local(): lax.all_to_all(jnp.take(shaped, mine, axis=0).reshape(rows, query.shape[1...]
    ppermute x31 -> x0, starting transfers between devices: 9.58 us -> none  [from_behind(): return lax.ppermute(block, axis, route)]
    reduce_sum x64 -> x0, other arithmetic: 9.48 us -> none  [the longest x32 6.65 us: attend(): total = total * keep + jnp.sum(weights, axis=-1)]
    and x33 -> x0, other arithmetic: 5.5 us -> none  [the longest x32 5.49 us: attend(): (kpos[None, :] >= 0) & (kpos[None, :] <= qpos[:, None])]
  transfers between devices with their start and end apart: 33 -> 0, of which waited for: 33 -> 0; matrix products, arithmetic and copies ran while one was open for 5% -> 0% of each run, Pallas kernels for 0% -> 0%
where the time goes in v1:
time: 111 us
  Pallas kernels  104 us (94%)
  local copies, waits for them, and re-layouts  6.44 us (6%)
    pallas_call x1, Pallas kernels, local(): pl.pallas_call(kernel, out_shape=jax.ShapeDtypeStruct((ROWS, GROUP * HD),...  104 us
    unnamed x13, local copies, waits for them, and re-layouts  6.44 us

profile of v1, /device:TPU:1, one launch (start us, length us, event | category | flops | bytes accessed | tf_op | source)
XLA Modules:
  0.0 111.0 jit_solution(17241308556629822231)
XLA Ops:
  0.0 0.0 copy-start.5
  0.0 0.1 maximum_bitcast_fusion.freq
  0.1 0.6 copy-done.5
  0.7 0.0 copy-start
  0.7 1.2 %copy-done = bf16[4096,128]{1,0:T(8,128)(2,1)S(1)} copy-done((bf16[4096,128]{1,0:T(8,128)(2,1)S(1)}, bf16[4096,128]{1,0:T(8,128)(2,1)}, u32[]{:S(2)}) %copy-start) | copy-done | bytes 1048600
  1.9 0.0 copy-start.1
  1.9 1.2 %copy-done.1 = bf16[4096,128]{1,0:T(8,128)(2,1)S(1)} copy-done((bf16[4096,128]{1,0:T(8,128)(2,1)S(1)}, bf16[4096,128]{1,0:T(8,128)(2,1)}, u32[]{:S(2)}) %copy-start.1) | copy-done | bytes 1048600
  3.1 0.0 copy-start.2
  3.1 1.0 copy-done.2
  4.2 0.0 copy-start.3
  4.2 0.9 copy-done.3
  5.1 0.0 copy-start.4
  5.1 0.7 copy-done.4
  5.8 104.4 %attend.1 = bf16[256,512]{1,0:T(8,128)(2,1)S(1)} custom-call(bf16[256,1024]{1,0:T(8,128)(2,1)S(1)} %copy-done.2, bf16[256,512]{1,0:T(8,128)(2,1)S(1)} %copy-done.3, bf16[4096,128]{1,0:T(8,128)(2,1)S(1)} %copy-done, bf16[4096,128]{1,0:T(8,128)(2,1)S(1)} %copy-done.1, s32[16]{0:T(128)S(1)} %copy-done.5, s32[32,32]{1,0:T(8,128)S(1)} %copy-done.4, ...), custom_call_target="tpu_custom_call" | custom-call | tf_op jit(solution)/shard_map/attend/pallas_call | solution.py:489
  110.3 0.7 copy.8
  (1 shorter events, 0.0 us)
Async XLA Ops:
  0.0 0.7 copy-start.5
  0.7 1.2 %copy-start = (bf16[4096,128]{1,0:T(8,128)(2,1)S(1)}, bf16[4096,128]{1,0:T(8,128)(2,1)}, u32[]{:S(2)}) copy-start(bf16[4096,128]{1,0:T(8,128)(2,1)} %w_key.1) | copy-start | bytes 3145732
  1.9 1.2 %copy-start.1 = (bf16[4096,128]{1,0:T(8,128)(2,1)S(1)}, bf16[4096,128]{1,0:T(8,128)(2,1)}, u32[]{:S(2)}) copy-start(bf16[4096,128]{1,0:T(8,128)(2,1)} %w_value.1) | copy-start | bytes 3145732
  3.1 1.0 copy-start.2
  4.2 0.9 copy-start.3
  5.1 0.7 copy-start.4

commit v2 on v1

v2 whole, which is shorter than its diff:
```python
import functools

import jax
import jax.numpy as jnp
import numpy as np
from jax import lax
from jax.experimental import pallas as pl
from jax.experimental.pallas import tpu as pltpu
from jax.sharding import PartitionSpec as P

HD = 128
GROUP = 4
ROWS = 256
BROW = 8
NCTX = 32
NHEAD = 4
NDOCS = 16
FEAT = 1024
BEHIND = 8
ROPE_BASE = 500000.0
MASKED = -1e30
MESH = pl.DeviceIdType.MESH

SHIFT = 2
CHUNKS = 8
DEPTH = 3
LAG_OPP = 3
LAG_HOP = 5

R = ROWS // CHUNKS
BACKWARD = SHIFT
FORWARD = BEHIND // 2 - SHIFT
GROUPS = CHUNKS // 2
OWN = BEHIND - 2 * SHIFT
QROWS = GROUP * ROWS
KEYS = 2 * BEHIND * R
BLOCK = GROUP * BROW
ROUNDS = NCTX // 4 - 1
EXPC = float(np.log2(np.e) / np.sqrt(HD))

F32 = jnp.float32
BF16 = jnp.bfloat16


def when(cond):
    if isinstance(cond, (bool, np.bool_)):
        return (lambda f: f()) if cond else (lambda f: None)
    return pl.when(cond)


def both(*conds):
    out = True
    for c in conds:
        if isinstance(c, (bool, np.bool_)):
            if not c:
                return False
        else:
            out = c if out is True else jnp.logical_and(out, c)
    return out


def kernel(
    tokens, query, w_key, w_value, lengths, balance, freq, out,
    gath, wkv, part, cosf, sinf, kv, kvd, qbuf, q2, qidx, mx, tot, acc, stage, recv,
    local_sem, tsend, trecv, zsend, zrecv, srecv, qsend, qrecv, osend, orecv, round_sem,
):
    x = lax.axis_index("dp")
    me = lax.axis_index("ctx")
    y = lax.axis_index("head")
    z = me // 2
    core = lax.rem(me, 2)
    up = lax.rem(y + 1, NHEAD)
    down = lax.rem(y + NHEAD - 1, NHEAD)
    opposite = lax.rem(y + 2, NHEAD)
    sibling = me + 1 - 2 * core
    qshard = lax.rem(me + 2 * SHIFT, NCTX)

    def remote(src, dst, ssem, rsem, ctx, head):
        return pltpu.make_async_remote_copy(
            src_ref=src, dst_ref=dst, send_sem=ssem, recv_sem=rsem,
            device_id=(x, ctx, head), device_id_type=MESH,
        )

    def own_copy(c, p):
        rows = pl.ds(c * R, R)
        return remote(
            tokens.at[rows, :], gath.at[1 + p, rows, :], tsend.at[0], trecv.at[p, c],
            me, up if p == 0 else down,
        )

    def relay_copy(c, p):
        rows = pl.ds(c * R + p * (R // 2), R // 2)
        return remote(
            gath.at[1 + p, rows, :], gath.at[3, rows, :], tsend.at[0], trecv.at[2 + p, c],
            me, up if p == 0 else down,
        )

    def slot(c, u):
        if u == BEHIND:
            return kvd.at[pl.ds(c * R, R), pl.ds(0, 2 * HD)]
        return kv.at[c // 2, pl.ds(lax.rem(c, 2) * (BEHIND * R) + u * R, R), pl.ds(0, 2 * HD)]

    def hop_copy(c, sign, h):
        index = h - 1 if sign > 0 else FORWARD + h - 1
        return remote(
            slot(c, OWN), slot(c, OWN - sign * 2 * h), zsend.at[0], zrecv.at[index, c],
            lax.rem(me + NCTX + sign * 2 * h, NCTX), y,
        )

    def sib_copy(c, u):
        there = pl.multiple_of(lax.rem(c, 2) * (BEHIND * R) + (u - 1 + 2 * core) * R, R)
        return remote(
            slot(c, u), kv.at[c // 2, pl.ds(there, R), pl.ds(0, 2 * HD)],
            zsend.at[0], srecv.at[u // 2 - 1 + core, c], sibling, y,
        )

    def sib_cond(u):
        if u == 0:
            return core == 1
        if u == BEHIND:
            return core == 0
        return True

    def sib_start(c, u):
        @when(sib_cond(u))
        def _():
            sib_copy(c, u).start()

    def sib_wait(c, k):
        remote(
            slot(c, 2 * k), slot(c, 2 * k + 1), zsend.at[0], srecv.at[k, c], sibling, y
        ).wait_recv()

    query_copy = remote(
        query, qbuf, qsend.at[0], qrecv.at[0], lax.rem(me + NCTX - 2 * SHIFT, NCTX), y
    )

    barrier = pltpu.get_barrier_semaphore()

    ahead = lax.rem(me + 2, NCTX)
    astern = lax.rem(me + NCTX - 2, NCTX)
    for ctx, head in ((me, up), (me, down), (ahead, y), (astern, y), (sibling, y)):
        pl.semaphore_signal(barrier, inc=1, device_id=(x, ctx, head), device_id_type=MESH)

    def tell(k):
        for ctx in (ahead, astern):
            pl.semaphore_signal(
                round_sem.at[k], inc=1, device_id=(x, ctx, y), device_id_type=MESH
            )

    loads = [
        pltpu.make_async_copy(tokens, gath.at[0], local_sem.at[0]),
        pltpu.make_async_copy(w_value, wkv.at[:, pl.ds(0, HD)], local_sem.at[1]),
        pltpu.make_async_copy(w_key, wkv.at[:, pl.ds(HD, HD)], local_sem.at[2]),
    ]
    if SHIFT == 0:
        loads.append(pltpu.make_async_copy(query, qbuf, local_sem.at[3]))
    for load in loads:
        load.start()

    pl.semaphore_wait(barrier, 5)

    for c in range(DEPTH):
        for p in range(2):
            own_copy(c, p).start()
    tell(0)

    lane = lax.broadcasted_iota(jnp.int32, (1, HD), 1)
    low = jnp.zeros((1, HD), jnp.int32)
    high = jnp.zeros((1, HD), jnp.int32)
    edge = jnp.int32(0)
    for j in range(NDOCS):
        low = jnp.where(lane == j, edge, low)
        edge = edge + lengths[j]
        high = jnp.where(lane == j, edge, high)

    def in_doc(pos):
        return (pos >= low) & (pos < high)

    pos = me * ROWS + lax.broadcasted_iota(jnp.int32, (ROWS, HD), 0)
    angle = pos.astype(F32) * freq[...]
    cosf[...] = jnp.cos(angle)
    sine = jnp.sin(angle)
    sinf[...] = jnp.where(lax.broadcasted_iota(jnp.int32, (ROWS, HD), 1) < HD // 2, -sine, sine)

    def mark(c, carry):
        row = lax.broadcasted_iota(jnp.int32, (BEHIND * R, HD), 0)
        shard = (me + NCTX - BEHIND + 2 * SHIFT + row // R) & (NCTX - 1)
        kpos = shard * ROWS + c * R + (row & (R - 1))
        half = pl.ds(pl.multiple_of(lax.rem(c, 2) * (BEHIND * R), BEHIND * R), BEHIND * R)
        kv[c // 2, half, pl.ds(2 * HD, HD)] = jnp.where(in_doc(kpos), 0.0, MASKED).astype(BF16)
        return carry

    lax.fori_loop(0, CHUNKS, mark, 0)
    qpos = qshard * ROWS + lax.broadcasted_iota(jnp.int32, (ROWS, HD), 0)
    kvd[:, pl.ds(2 * HD, HD)] = jnp.where(in_doc(qpos), 0.0, MASKED).astype(BF16)

    mx[...] = jnp.full_like(mx, MASKED)
    tot[...] = jnp.zeros_like(tot)
    acc[...] = jnp.zeros_like(acc)
    for load in loads:
        load.wait()

    def dest_of(n, e):
        if isinstance(n, int):
            dz = 8 - n if e < 2 else (0 if n == 0 else n - 8)
        else:
            dz = 8 - n if e < 2 else jnp.where(n == 0, 0, n - 8)
        return ((z + 16 + dz) & 15) * 2 + ((core + e) & 1)

    def prepare_query():
        if SHIFT:
            query_copy.wait_recv()
        r = lax.broadcasted_iota(jnp.int32, (ROWS, NCTX), 0)
        n = r >> 5
        e = (r >> 3) & 3
        dz = jnp.where(e < 2, 8 - n, jnp.where(n == 0, 0, n - 8))
        dest = ((z + 16 + dz) & 15) * 2 + ((core + e) & 1)
        bal = balance[pl.ds(qshard, 1), :]
        pick = jnp.where(bal == dest, 1.0, 0.0).astype(BF16)
        b = lax.broadcasted_iota(jnp.int32, (NCTX, ROWS), 0)
        c = lax.broadcasted_iota(jnp.int32, (NCTX, ROWS), 1)
        widen = jnp.where((c >> 3) == b, 1.0, 0.0).astype(BF16)
        spread = jnp.dot(pick, widen, preferred_element_type=F32)
        r = lax.broadcasted_iota(jnp.int32, (ROWS, ROWS), 0)
        c = lax.broadcasted_iota(jnp.int32, (ROWS, ROWS), 1)
        perm = jnp.where((c & 7) == (r & 7), spread, 0.0).astype(BF16)
        moved = jnp.dot(perm, qbuf[...], preferred_element_type=F32)
        doc = jnp.where(in_doc(qpos), 1.0, 0.0).astype(BF16)
        doc = jnp.dot(perm, doc, preferred_element_type=F32)
        index = lax.broadcasted_iota(jnp.int32, (ROWS, HD), 0).astype(F32).astype(BF16)
        index = jnp.dot(perm, index, preferred_element_type=F32)

        def rows_of(parts):
            parts = [p.reshape(NCTX, BROW, HD) for p in parts]
            return jnp.stack(parts, axis=1).reshape(QROWS, HD)

        q2[:, pl.ds(0, HD)] = rows_of(
            [moved[:, g * HD : (g + 1) * HD] for g in range(GROUP)]
        ).astype(BF16)
        q2[:, pl.ds(HD, HD)] = rows_of([doc] * GROUP).astype(BF16)
        qidx[...] = rows_of([index] * GROUP)

    def nt(a, b):
        return lax.dot_general(a, b, (((1,), (1,)), ((), ())), preferred_element_type=F32)

    def update(score, values):
        width = score.shape[1]
        old = mx[...]
        new = jnp.maximum(old, jnp.max(score, axis=1, keepdims=True))
        keep = jnp.exp2((old - new) * EXPC)
        wide = jnp.concatenate([new] * (width // HD), axis=1) if width > HD else new
        weight = jnp.exp2((score - wide) * EXPC)
        lanes = weight[:, :HD]
        for k in range(1, width // HD):
            lanes = lanes + weight[:, k * HD : (k + 1) * HD]
        mx[...] = new
        tot[...] = tot[...] * keep + lanes
        acc[...] = acc[...] * keep + jnp.dot(
            weight.astype(BF16), values, preferred_element_type=F32
        )

    def plain(g):
        update(nt(q2[...], kv[g, :, pl.ds(HD, 2 * HD)]), kv[g, :, pl.ds(0, HD)])

    def diagonal(half):
        keys = pl.ds(pl.multiple_of(half * HD, HD), HD)
        score = nt(q2[...], kvd[keys, pl.ds(HD, 2 * HD)])
        kidx = (half * HD + lax.broadcasted_iota(jnp.int32, (QROWS, HD), 1)).astype(F32)
        update(jnp.where(kidx <= qidx[...], score, MASKED), kvd[keys, pl.ds(0, HD)])

    def out_copy(n, e):
        rows = pl.ds(pl.multiple_of((n * 4 + e) * BLOCK, BLOCK), BLOCK)
        there = pl.ds(pl.multiple_of(qshard * BLOCK, BLOCK), BLOCK)
        return remote(
            stage.at[rows, :], recv.at[there, :], osend.at[0], orecv.at[qshard],
            dest_of(n, e), y,
        )

    def hops(c):
        for sign, count in ((1, FORWARD), (-1, BACKWARD)):
            for h in range(1, count + 1):
                hop_copy(c, sign, h).wait_recv()
                sib_start(c, OWN - sign * 2 * h)

    def sib_arrived(g):
        for c in (2 * g, 2 * g + 1):
            for k in range(4):
                sib_wait(c, k)

    def finish(c):
        rows = pl.ds(c * R, R)
        for p in range(2):
            relay_copy(c, p).wait_recv()
        raw = part[rows, :] + jnp.dot(
            gath[3, rows, :], wkv[pl.ds(pl.multiple_of(opposite * FEAT, FEAT), FEAT), :],
            preferred_element_type=F32,
        )
        value = raw[:, :HD]
        key = raw[:, HD:]
        key = key * cosf[rows, :] + pltpu.roll(key, HD // 2, 1) * sinf[rows, :]
        slot(c, OWN)[...] = jnp.concatenate([value, key], axis=1).astype(BF16)
        for sign, count in ((1, FORWARD), (-1, BACKWARD)):
            for h in range(1, count + 1):
                hop_copy(c, sign, h).start()
        sib_start(c, OWN)

    def gather(i, carry):
        for p in range(2):
            own_copy(i, p).wait_recv()
            relay_copy(i, p).start()

        @pl.when(i + DEPTH < CHUNKS)
        def _():
            for p in range(2):
                own_copy(i + DEPTH, p).start()

        rows = pl.ds(i * R, R)
        total = None
        for s, source in enumerate((y, down, up)):
            term = jnp.dot(
                gath[s, rows, :], wkv[pl.ds(pl.multiple_of(source * FEAT, FEAT), FEAT), :],
                preferred_element_type=F32,
            )
            total = term if total is None else total + term
        part[rows, :] = total

        @pl.when(i >= LAG_OPP)
        def _():
            finish(i - LAG_OPP)

        @pl.when(i >= LAG_HOP)
        def _():
            hops(i - LAG_HOP)

        @pl.when(i < ROUNDS)
        def _():
            pl.semaphore_wait(round_sem.at[i], 2)

        @pl.when(i < ROUNDS - 1)
        def _():
            tell(i + 1)

        if SHIFT:
            @pl.when(i == 0)
            def _():
                query_copy.start()

        @pl.when(i == ROUNDS)
        def _():
            pl.semaphore_signal(
                round_sem.at[ROUNDS], inc=1, device_id=(x, sibling, y), device_id_type=MESH
            )
            pl.semaphore_wait(round_sem.at[ROUNDS], 1)

        return carry

    lax.fori_loop(0, CHUNKS, gather, 0)
    prepare_query()

    def finish_loop(c, carry):
        finish(c)
        return carry

    def hops_loop(c, carry):
        hops(c)
        return carry

    lax.fori_loop(CHUNKS - LAG_OPP, CHUNKS, finish_loop, 0)
    lax.fori_loop(CHUNKS - LAG_HOP, CHUNKS - 3, hops_loop, 0)

    def attend(g, carry):
        sib_arrived(g)
        plain(g)

        @pl.when(lax.rem(g, 2) == 1)
        def _():
            diagonal(g // 2)

        @pl.when(g < GROUPS - 1)
        def _():
            hops(g + CHUNKS - 3)

        return carry

    lax.fori_loop(0, GROUPS, attend, 0)

    total = jnp.sum(tot[...], axis=1, keepdims=True)
    stage[...] = (acc[...] / total).astype(BF16)

    def send(rb, carry):
        for e in range(4):
            if e == 2:
                @pl.when(rb > 0)
                def _():
                    out_copy(rb, e).start()
            else:
                out_copy(rb, e).start()
        return carry

    lax.fori_loop(0, QROWS // (4 * BLOCK), send, 0)

    def sent(block, sem):
        pltpu.make_async_copy(block, block, sem).wait()

    sent(gath.at[pl.ds(0, 3)], tsend.at[0])
    sent(gath.at[pl.ds(0, 2)], zsend.at[0])
    if SHIFT:
        query_copy.wait_send()

    def arrive(dz, own):
        source = (z + 16 + dz) & 15
        chip = (source + SHIFT) & 15
        for k in range(2):
            shard = chip * 2 + k
            there = pl.ds(pl.multiple_of(shard * BLOCK, BLOCK), BLOCK)

            def landed():
                remote(
                    stage.at[pl.ds(0, BLOCK), :], recv.at[there, :], osend.at[0], orecv.at[shard],
                    sibling, y,
                ).wait_recv()

            if own:
                pl.when(core != k)(landed)
            else:
                landed()
        if own:
            there = pl.ds(pl.multiple_of(qshard * BLOCK, BLOCK), BLOCK)
            recv[there, :] = stage[pl.ds(2 * BLOCK, BLOCK), :]
        block = recv[pl.ds(pl.multiple_of(chip * 2 * BLOCK, 2 * BLOCK), 2 * BLOCK), :].astype(F32)
        heads = [
            jnp.concatenate(
                [
                    block[g * BROW : (g + 1) * BROW],
                    block[BLOCK + g * BROW : BLOCK + (g + 1) * BROW],
                ],
                axis=0,
            )
            for g in range(GROUP)
        ]
        out[pl.ds(pl.multiple_of(chip * 2 * BROW, 2 * BROW), 2 * BROW), :] = jnp.concatenate(
            heads, axis=1
        ).astype(BF16)

    arrive(0, True)
    arrive(8, False)

    def pair(n, carry):
        arrive(8 - n, False)
        arrive(n - 8, False)
        return carry

    lax.fori_loop(1, 8, pair, 0)

    sent(stage.at[pl.ds(0, QROWS - BLOCK), :], osend.at[0])


def local(tokens, query, w_key, w_value, doc_lengths, balance):
    half = HD // 2
    freq = ROPE_BASE ** (-(jnp.arange(half, dtype=F32) * 2.0 / HD))
    freq = jnp.concatenate([freq, freq])[None, :]
    hbm = pl.BlockSpec(memory_space=pltpu.HBM)
    vmem = pl.BlockSpec(memory_space=pltpu.VMEM)
    smem = pl.BlockSpec(memory_space=pltpu.SMEM)
    dma = pltpu.SemaphoreType.DMA
    width = 2 * HD
    return pl.pallas_call(
        kernel,
        out_shape=jax.ShapeDtypeStruct((ROWS, GROUP * HD), BF16),
        in_specs=[hbm, hbm, hbm, hbm, smem, vmem, vmem],
        out_specs=vmem,
        scratch_shapes=[
            pltpu.VMEM((NHEAD, ROWS, FEAT), BF16),
            pltpu.VMEM((NHEAD * FEAT, width), BF16),
            pltpu.VMEM((ROWS, width), F32),
            pltpu.VMEM((ROWS, HD), F32),
            pltpu.VMEM((ROWS, HD), F32),
            pltpu.VMEM((GROUPS, KEYS, 3 * HD), BF16),
            pltpu.VMEM((ROWS, 3 * HD), BF16),
            pltpu.VMEM((ROWS, GROUP * HD), BF16),
            pltpu.VMEM((QROWS, width), BF16),
            pltpu.VMEM((QROWS, HD), F32),
            pltpu.VMEM((QROWS, HD), F32),
            pltpu.VMEM((QROWS, HD), F32),
            pltpu.VMEM((QROWS, HD), F32),
            pltpu.VMEM((QROWS, HD), BF16),
            pltpu.VMEM((QROWS, HD), BF16),
            dma((4,)),
            dma((1,)),
            dma((4, CHUNKS)),
            dma((1,)),
            dma((FORWARD + BACKWARD, CHUNKS)),
            dma((4, CHUNKS)),
            dma((1,)),
            dma((1,)),
            dma((1,)),
            dma((NCTX,)),
            pltpu.SemaphoreType.REGULAR((ROUNDS + 1,)),
        ],
        compiler_params=pltpu.CompilerParams(
            collective_id=0, has_side_effects=True, vmem_limit_bytes=60 * 1024 * 1024
        ),
        name="attend",
    )(tokens, query, w_key, w_value, doc_lengths, balance, freq)


def solution(mesh):
    placed = (
        P(("dp", "ctx"), "head"),
        P(("dp", "ctx"), "head"),
        P(None, "head"),
        P(None, "head"),
        P("dp"),
        P("dp", None),
    )
    return jax.shard_map(
        local, mesh=mesh, in_specs=placed, out_specs=P(("dp", "ctx"), "head"), check_vma=False
    )
```

time: 111 us -> 63.3 us (0.57)
  Pallas kernels: 104 us -> 60.8 us
  local copies, waits for them, and re-layouts: 6.44 us -> 1.67 us
    pallas_call x1, Pallas kernels: 104 us -> 60.8 us  [local(): pl.pallas_call(kernel, out_shape=jax.ShapeDtypeStruct((ROWS, GROUP * HD),...]
    unnamed x13 -> x1, local copies, waits for them, and re-layouts: 6.44 us -> 1.67 us
where the time goes in v2:
time: 63.3 us; the launch traced here: 63.1 us
  Pallas kernels  60.8 us (96%)
  local copies, waits for them, and re-layouts  1.67 us (3%)
    pallas_call x1, Pallas kernels, local(): pl.pallas_call(kernel, out_shape=jax.ShapeDtypeStruct((ROWS, GROUP * HD),...  60.8 us
    unnamed x1, local copies, waits for them, and re-layouts  1.67 us

profile of v2, /device:TPU:1, one launch (start us, length us, event | category | flops | bytes accessed | tf_op | source)
XLA Modules:
  0.0 63.1 jit_solution(11469130037535297818)
XLA Ops:
  0.0 0.6 maximum_bitcast_fusion.freq
  0.6 60.8 %attend.1 = bf16[256,512]{1,0:T(8,128)(2,1)} custom-call(bf16[256,1024]{1,0:T(8,128)(2,1)} %tokens.1, bf16[256,512]{1,0:T(8,128)(2,1)} %query.1, bf16[4096,128]{1,0:T(8,128)(2,1)} %w_key.1, bf16[4096,128]{1,0:T(8,128)(2,1)} %w_value.1, s32[16]{0:T(128)} %lengths.1, s32[32,32]{1,0:T(8,128)} %balance.1, f32[1,128]{1,0:T(1,128)} %maximum_bitcast_fusion.freq), custom_call_target="tpu_custom_call" | custom-call | tf_op jit(solution)/shard_map/attend/pallas_call | solution.py:468
  61.4 1.7 %copy.8 = bf16[256,512]{1,0:T(8,128)(2,1)} copy(bf16[256,512]{1,0:T(8,128)(2,1)} %attend.1) | data formatting | bytes 524288
  (1 shorter events, 0.0 us)

commit v3 on v2

--- a/solution.py
+++ b/solution.py
@@ -23,9 +23,8 @@
 
 SHIFT = 2
 CHUNKS = 8
-DEPTH = 3
+DEPTH = 4
 LAG_OPP = 3
-LAG_HOP = 5
 
 R = ROWS // CHUNKS
 BACKWARD = SHIFT
@@ -33,7 +32,8 @@
 GROUPS = CHUNKS // 2
 OWN = BEHIND - 2 * SHIFT
 QROWS = GROUP * ROWS
-KEYS = 2 * BEHIND * R
+GROWS = 2 * R
+PARTS = 2
 BLOCK = GROUP * BROW
 ROUNDS = NCTX // 4 - 1
 EXPC = float(np.log2(np.e) / np.sqrt(HD))
@@ -61,7 +61,7 @@
 
 def kernel(
     tokens, query, w_key, w_value, lengths, balance, freq, out,
-    gath, wkv, part, cosf, sinf, kv, kvd, qbuf, q2, qidx, mx, tot, acc, stage, recv,
+    gath, wkv, part, cosf, sinf, kv, qbuf, q2, qidx, mx, tot, acc, stage, recv,
     local_sem, tsend, trecv, zsend, zrecv, srecv, qsend, qrecv, osend, orecv, round_sem,
 ):
     x = lax.axis_index("dp")
@@ -95,41 +95,47 @@
             me, up if p == 0 else down,
         )
 
-    def slot(c, u):
-        if u == BEHIND:
-            return kvd.at[pl.ds(c * R, R), pl.ds(0, 2 * HD)]
-        return kv.at[c // 2, pl.ds(lax.rem(c, 2) * (BEHIND * R) + u * R, R), pl.ds(0, 2 * HD)]
+    def slot(u, start, size):
+        return kv.at[u, pl.ds(pl.multiple_of(start, size), size), pl.ds(0, 2 * HD)]
 
     def hop_copy(c, sign, h):
         index = h - 1 if sign > 0 else FORWARD + h - 1
         return remote(
-            slot(c, OWN), slot(c, OWN - sign * 2 * h), zsend.at[0], zrecv.at[index, c],
-            lax.rem(me + NCTX + sign * 2 * h, NCTX), y,
-        )
-
-    def sib_copy(c, u):
-        there = pl.multiple_of(lax.rem(c, 2) * (BEHIND * R) + (u - 1 + 2 * core) * R, R)
-        return remote(
-            slot(c, u), kv.at[c // 2, pl.ds(there, R), pl.ds(0, 2 * HD)],
-            zsend.at[0], srecv.at[u // 2 - 1 + core, c], sibling, y,
-        )
-
-    def sib_cond(u):
+            slot(OWN, c * R, R), slot(OWN - sign * 2 * h, c * R, R),
+            zsend.at[0], zrecv.at[index, c // 2], lax.rem(me + NCTX + sign * 2 * h, NCTX), y,
+        )
+
+    def hop_wait(g, sign, h):
+        index = h - 1 if sign > 0 else FORWARD + h - 1
+        here = slot(OWN - sign * 2 * h, g * GROWS, GROWS)
+        pltpu.make_async_copy(here, here, zrecv.at[index, g]).wait()
+
+    def sib_start(g, u):
+        def start():
+            remote(
+                slot(u, g * GROWS, GROWS), slot(u - 1 + 2 * core, g * GROWS, GROWS),
+                zsend.at[0], srecv.at[u // 2 - 1 + core, g], sibling, y,
+            ).start()
+
         if u == 0:
-            return core == 1
-        if u == BEHIND:
-            return core == 0
-        return True
-
-    def sib_start(c, u):
-        @when(sib_cond(u))
-        def _():
-            sib_copy(c, u).start()
-
-    def sib_wait(c, k):
-        remote(
-            slot(c, 2 * k), slot(c, 2 * k + 1), zsend.at[0], srecv.at[k, c], sibling, y
-        ).wait_recv()
+            pl.when(core == 1)(start)
+        elif u == BEHIND:
+            pl.when(core == 0)(start)
+        else:
+            start()
+
+    def sib_arrived(g):
+        for k in range(BEHIND // 2):
+            here = slot(2 * k + 1, g * GROWS, GROWS)
+            pltpu.make_async_copy(here, here, srecv.at[k, g]).wait()
+
+    def hops(g):
+        sib_start(g, OWN)
+        for h in range(1, max(FORWARD, BACKWARD) + 1):
+            for sign, count in ((1, FORWARD), (-1, BACKWARD)):
+                if h <= count:
+                    hop_wait(g, sign, h)
+                    sib_start(g, OWN - sign * 2 * h)
 
     query_copy = remote(
         query, qbuf, qsend.at[0], qrecv.at[0], lax.rem(me + NCTX - 2 * SHIFT, NCTX), y
@@ -183,17 +189,14 @@
     sine = jnp.sin(angle)
     sinf[...] = jnp.where(lax.broadcasted_iota(jnp.int32, (ROWS, HD), 1) < HD // 2, -sine, sine)
 
-    def mark(c, carry):
-        row = lax.broadcasted_iota(jnp.int32, (BEHIND * R, HD), 0)
-        shard = (me + NCTX - BEHIND + 2 * SHIFT + row // R) & (NCTX - 1)
-        kpos = shard * ROWS + c * R + (row & (R - 1))
-        half = pl.ds(pl.multiple_of(lax.rem(c, 2) * (BEHIND * R), BEHIND * R), BEHIND * R)
-        kv[c // 2, half, pl.ds(2 * HD, HD)] = jnp.where(in_doc(kpos), 0.0, MASKED).astype(BF16)
+    def mark(u, carry):
+        shard = (me + NCTX - BEHIND + 2 * SHIFT + u) & (NCTX - 1)
+        kpos = shard * ROWS + lax.broadcasted_iota(jnp.int32, (ROWS, HD), 0)
+        kv[u, :, pl.ds(2 * HD, HD)] = jnp.where(in_doc(kpos), 0.0, MASKED).astype(BF16)
         return carry
 
-    lax.fori_loop(0, CHUNKS, mark, 0)
+    lax.fori_loop(0, BEHIND + 1, mark, 0)
     qpos = qshard * ROWS + lax.broadcasted_iota(jnp.int32, (ROWS, HD), 0)
-    kvd[:, pl.ds(2 * HD, HD)] = jnp.where(in_doc(qpos), 0.0, MASKED).astype(BF16)
 
     mx[...] = jnp.full_like(mx, MASKED)
     tot[...] = jnp.zeros_like(tot)
@@ -244,30 +247,34 @@
     def nt(a, b):
         return lax.dot_general(a, b, (((1,), (1,)), ((), ())), preferred_element_type=F32)
 
-    def update(score, values):
+    def attend(g, rows):
+        group = pl.ds(g * GROWS, GROWS)
+        keys = kv[pl.ds(0, BEHIND), group, pl.ds(HD, 2 * HD)].reshape(BEHIND * GROWS, 2 * HD)
+        values = kv[pl.ds(0, BEHIND), group, pl.ds(0, HD)].reshape(BEHIND * GROWS, HD)
+        if g % 2:
+            start = g // 2 * HD
+            half = pl.ds(start, HD)
+            keys = jnp.concatenate([keys, kv[BEHIND, half, pl.ds(HD, 2 * HD)]], axis=0)
+            values = jnp.concatenate([values, kv[BEHIND, half, pl.ds(0, HD)]], axis=0)
+        score = nt(q2[rows, :], keys)
         width = score.shape[1]
-        old = mx[...]
+        if g % 2:
+            index = qidx[rows, :]
+            kidx = (start + lax.broadcasted_iota(jnp.int32, index.shape, 1)).astype(F32)
+            last = jnp.where(kidx <= index, score[:, width - HD :], MASKED)
+            score = jnp.concatenate([score[:, : width - HD], last], axis=1)
+        old = mx[rows, :]
         new = jnp.maximum(old, jnp.max(score, axis=1, keepdims=True))
         keep = jnp.exp2((old - new) * EXPC)
-        wide = jnp.concatenate([new] * (width // HD), axis=1) if width > HD else new
-        weight = jnp.exp2((score - wide) * EXPC)
+        weight = jnp.exp2((score - jnp.concatenate([new] * (width // HD), axis=1)) * EXPC)
         lanes = weight[:, :HD]
         for k in range(1, width // HD):
             lanes = lanes + weight[:, k * HD : (k + 1) * HD]
-        mx[...] = new
-        tot[...] = tot[...] * keep + lanes
-        acc[...] = acc[...] * keep + jnp.dot(
+        mx[rows, :] = new
+        tot[rows, :] = tot[rows, :] * keep + lanes
+        acc[rows, :] = acc[rows, :] * keep + jnp.dot(
             weight.astype(BF16), values, preferred_element_type=F32
         )
-
-    def plain(g):
-        update(nt(q2[...], kv[g, :, pl.ds(HD, 2 * HD)]), kv[g, :, pl.ds(0, HD)])
-
-    def diagonal(half):
-        keys = pl.ds(pl.multiple_of(half * HD, HD), HD)
-        score = nt(q2[...], kvd[keys, pl.ds(HD, 2 * HD)])
-        kidx = (half * HD + lax.broadcasted_iota(jnp.int32, (QROWS, HD), 1)).astype(F32)
-        update(jnp.where(kidx <= qidx[...], score, MASKED), kvd[keys, pl.ds(0, HD)])
 
     def out_copy(n, e):
         rows = pl.ds(pl.multiple_of((n * 4 + e) * BLOCK, BLOCK), BLOCK)
@@ -276,17 +283,6 @@
             stage.at[rows, :], recv.at[there, :], osend.at[0], orecv.at[qshard],
             dest_of(n, e), y,
         )
-
-    def hops(c):
-        for sign, count in ((1, FORWARD), (-1, BACKWARD)):
-            for h in range(1, count + 1):
-                hop_copy(c, sign, h).wait_recv()
-                sib_start(c, OWN - sign * 2 * h)
-
-    def sib_arrived(g):
-        for c in (2 * g, 2 * g + 1):
-            for k in range(4):
-                sib_wait(c, k)
 
     def finish(c):
         rows = pl.ds(c * R, R)
@@ -299,11 +295,10 @@
         value = raw[:, :HD]
         key = raw[:, HD:]
         key = key * cosf[rows, :] + pltpu.roll(key, HD // 2, 1) * sinf[rows, :]
-        slot(c, OWN)[...] = jnp.concatenate([value, key], axis=1).astype(BF16)
+        kv[OWN, rows, pl.ds(0, 2 * HD)] = jnp.concatenate([value, key], axis=1).astype(BF16)
         for sign, count in ((1, FORWARD), (-1, BACKWARD)):
             for h in range(1, count + 1):
                 hop_copy(c, sign, h).start()
-        sib_start(c, OWN)
 
     def gather(i, carry):
         for p in range(2):
@@ -329,10 +324,6 @@
         def _():
             finish(i - LAG_OPP)
 
-        @pl.when(i >= LAG_HOP)
-        def _():
-            hops(i - LAG_HOP)
-
         @pl.when(i < ROUNDS)
         def _():
             pl.semaphore_wait(round_sem.at[i], 2)
@@ -362,31 +353,20 @@
         finish(c)
         return carry
 
-    def hops_loop(c, carry):
-        hops(c)
-        return carry
-
-    lax.fori_loop(CHUNKS - LAG_OPP, CHUNKS, finish_loop, 0)
-    lax.fori_loop(CHUNKS - LAG_HOP, CHUNKS - 3, hops_loop, 0)
-
-    def attend(g, carry):
-        sib_arrived(g)
-        plain(g)
-
-        @pl.when(lax.rem(g, 2) == 1)
-        def _():
-            diagonal(g // 2)
-
-        @pl.when(g < GROUPS - 1)
-        def _():
-            hops(g + CHUNKS - 3)
-
-        return carry
-
-    lax.fori_loop(0, GROUPS, attend, 0)
-
-    total = jnp.sum(tot[...], axis=1, keepdims=True)
-    stage[...] = (acc[...] / total).astype(BF16)
+    every = pl.ds(0, QROWS)
+    lax.fori_loop(CHUNKS - LAG_OPP, CHUNKS - 1, finish_loop, 0)
+    hops(0)
+    finish(CHUNKS - 1)
+    hops(1)
+    sib_arrived(0)
+    attend(0, every)
+    hops(2)
+    sib_arrived(1)
+    attend(1, every)
+    hops(3)
+    sib_arrived(2)
+    attend(2, every)
+    sib_arrived(3)
 
     def send(rb, carry):
         for e in range(4):
@@ -398,7 +378,12 @@
                 out_copy(rb, e).start()
         return carry
 
-    lax.fori_loop(0, QROWS // (4 * BLOCK), send, 0)
+    for p in range(PARTS):
+        rows = pl.ds(p * (QROWS // PARTS), QROWS // PARTS)
+        attend(3, rows)
+        total = jnp.sum(tot[rows, :], axis=1, keepdims=True)
+        stage[rows, :] = (acc[rows, :] / total).astype(BF16)
+        lax.fori_loop(p * (8 // PARTS), (p + 1) * (8 // PARTS), send, 0)
 
     def sent(block, sem):
         pltpu.make_async_copy(block, block, sem).wait()
@@ -476,8 +461,7 @@
             pltpu.VMEM((ROWS, width), F32),
             pltpu.VMEM((ROWS, HD), F32),
             pltpu.VMEM((ROWS, HD), F32),
-            pltpu.VMEM((GROUPS, KEYS, 3 * HD), BF16),
-            pltpu.VMEM((ROWS, 3 * HD), BF16),
+            pltpu.VMEM((BEHIND + 1, ROWS, 3 * HD), BF16),
             pltpu.VMEM((ROWS, GROUP * HD), BF16),
             pltpu.VMEM((QROWS, width), BF16),
             pltpu.VMEM((QROWS, HD), F32),
@@ -490,8 +474,8 @@
             dma((1,)),
             dma((4, CHUNKS)),
             dma((1,)),
-            dma((FORWARD + BACKWARD, CHUNKS)),
-            dma((4, CHUNKS)),
+            dma((FORWARD + BACKWARD, GROUPS)),
+            dma((BEHIND // 2, GROUPS)),
             dma((1,)),
             dma((1,)),
             dma((1,)),

time: 63.3 us -> 58.9 us (0.930)
  Pallas kernels: 60.8 us -> 56.4 us
    pallas_call x1, Pallas kernels: 60.8 us -> 56.4 us  [local(): pl.pallas_call(kernel, out_shape=jax.ShapeDtypeStruct((ROWS, GROUP * HD),...]
where the time goes in v3:
time: 58.9 us; the launch traced here: 58.7 us
  Pallas kernels  56.4 us (96%)
  local copies, waits for them, and re-layouts  1.67 us (3%)
  other arithmetic  0.6 us (1%)
    pallas_call x1, Pallas kernels, local(): pl.pallas_call(kernel, out_shape=jax.ShapeDtypeStruct((ROWS, GROUP * HD),...  56.4 us
    unnamed x1, local copies, waits for them, and re-layouts  1.67 us

profile of v3, /device:TPU:1, one launch (start us, length us, event | category | flops | bytes accessed | tf_op | source)
XLA Modules:
  0.0 58.7 jit_solution(5767940994808531534)
XLA Ops:
  0.0 0.6 %maximum_bitcast_fusion.freq = f32[1,128]{1,0:T(1,128)} fusion(f32[64]{0:T(128)S(1)} %negate_power_fusion), kind=kLoop, calls=%fused_computation | loop fusion | flops 128 | bytes 768 | tf_op jit(solution)/shard_map/broadcast_in_dim | solution.py:447
  0.6 56.4 %attend.1 = bf16[256,512]{1,0:T(8,128)(2,1)} custom-call(bf16[256,1024]{1,0:T(8,128)(2,1)} %tokens.1, bf16[256,512]{1,0:T(8,128)(2,1)} %query.1, bf16[4096,128]{1,0:T(8,128)(2,1)} %w_key.1, bf16[4096,128]{1,0:T(8,128)(2,1)} %w_value.1, s32[16]{0:T(128)} %lengths.1, s32[32,32]{1,0:T(8,128)} %balance.1, f32[1,128]{1,0:T(1,128)} %maximum_bitcast_fusion.freq), custom_call_target="tpu_custom_call" | custom-call | tf_op jit(solution)/shard_map/attend/pallas_call | solution.py:453
  57.1 1.7 %copy.8 = bf16[256,512]{1,0:T(8,128)(2,1)} copy(bf16[256,512]{1,0:T(8,128)(2,1)} %attend.1) | data formatting | bytes 524288
  (1 shorter events, 0.0 us)

commit v4 on v3

--- a/solution.py
+++ b/solution.py
@@ -36,6 +36,7 @@
 PARTS = 2
 BLOCK = GROUP * BROW
 ROUNDS = NCTX // 4 - 1
+FREQS = (ROPE_BASE ** (-(np.arange(HD // 2) * 2.0 / HD))).astype(np.float32)
 EXPC = float(np.log2(np.e) / np.sqrt(HD))
 
 F32 = jnp.float32
@@ -60,9 +61,9 @@
 
 
 def kernel(
-    tokens, query, w_key, w_value, lengths, balance, freq, out,
+    tokens, query, w_key, w_value, lengths_hbm, balance_hbm, out,
     gath, wkv, part, cosf, sinf, kv, qbuf, q2, qidx, mx, tot, acc, stage, recv,
-    local_sem, tsend, trecv, zsend, zrecv, srecv, qsend, qrecv, osend, orecv, round_sem,
+    local_sem, tsend, trecv, zsend, zrecv, srecv, qsend, qrecv, osend, orecv, round_sem, outv, lengths, balance,
 ):
     x = lax.axis_index("dp")
     me = lax.axis_index("ctx")
@@ -155,6 +156,8 @@
             )
 
     loads = [
+        pltpu.make_async_copy(lengths_hbm, lengths, local_sem.at[4]),
+        pltpu.make_async_copy(balance_hbm, balance, local_sem.at[5]),
         pltpu.make_async_copy(tokens, gath.at[0], local_sem.at[0]),
         pltpu.make_async_copy(w_value, wkv.at[:, pl.ds(0, HD)], local_sem.at[1]),
         pltpu.make_async_copy(w_key, wkv.at[:, pl.ds(HD, HD)], local_sem.at[2]),
@@ -171,6 +174,8 @@
             own_copy(c, p).start()
     tell(0)
 
+    for load in loads[:2]:
+        load.wait()
     lane = lax.broadcasted_iota(jnp.int32, (1, HD), 1)
     low = jnp.zeros((1, HD), jnp.int32)
     high = jnp.zeros((1, HD), jnp.int32)
@@ -184,7 +189,10 @@
         return (pos >= low) & (pos < high)
 
     pos = me * ROWS + lax.broadcasted_iota(jnp.int32, (ROWS, HD), 0)
-    angle = pos.astype(F32) * freq[...]
+    freq = jnp.zeros((1, HD), F32)
+    for j in range(HD // 2):
+        freq = jnp.where((lane & (HD // 2 - 1)) == j, float(FREQS[j]), freq)
+    angle = pos.astype(F32) * freq
     cosf[...] = jnp.cos(angle)
     sine = jnp.sin(angle)
     sinf[...] = jnp.where(lax.broadcasted_iota(jnp.int32, (ROWS, HD), 1) < HD // 2, -sine, sine)
@@ -201,7 +209,7 @@
     mx[...] = jnp.full_like(mx, MASKED)
     tot[...] = jnp.zeros_like(tot)
     acc[...] = jnp.zeros_like(acc)
-    for load in loads:
+    for load in loads[2:]:
         load.wait()
 
     def dest_of(n, e):
@@ -424,9 +432,9 @@
             )
             for g in range(GROUP)
         ]
-        out[pl.ds(pl.multiple_of(chip * 2 * BROW, 2 * BROW), 2 * BROW), :] = jnp.concatenate(
-            heads, axis=1
-        ).astype(BF16)
+        final = pl.ds(pl.multiple_of(chip * 2 * BROW, 2 * BROW), 2 * BROW)
+        outv[final, :] = jnp.concatenate(heads, axis=1).astype(BF16)
+        pltpu.make_async_copy(outv.at[final, :], out.at[final, :], local_sem.at[3]).start()
 
     arrive(0, True)
     arrive(8, False)
@@ -439,22 +447,18 @@
     lax.fori_loop(1, 8, pair, 0)
 
     sent(stage.at[pl.ds(0, QROWS - BLOCK), :], osend.at[0])
+    sent(outv, local_sem.at[3])
 
 
 def local(tokens, query, w_key, w_value, doc_lengths, balance):
-    half = HD // 2
-    freq = ROPE_BASE ** (-(jnp.arange(half, dtype=F32) * 2.0 / HD))
-    freq = jnp.concatenate([freq, freq])[None, :]
     hbm = pl.BlockSpec(memory_space=pltpu.HBM)
-    vmem = pl.BlockSpec(memory_space=pltpu.VMEM)
-    smem = pl.BlockSpec(memory_space=pltpu.SMEM)
     dma = pltpu.SemaphoreType.DMA
     width = 2 * HD
     return pl.pallas_call(
         kernel,
         out_shape=jax.ShapeDtypeStruct((ROWS, GROUP * HD), BF16),
-        in_specs=[hbm, hbm, hbm, hbm, smem, vmem, vmem],
-        out_specs=vmem,
+        in_specs=[hbm] * 6,
+        out_specs=hbm,
         scratch_shapes=[
             pltpu.VMEM((NHEAD, ROWS, FEAT), BF16),
             pltpu.VMEM((NHEAD * FEAT, width), BF16),
@@ -470,7 +474,7 @@
             pltpu.VMEM((QROWS, HD), F32),
             pltpu.VMEM((QROWS, HD), BF16),
             pltpu.VMEM((QROWS, HD), BF16),
-            dma((4,)),
+            dma((6,)),
             dma((1,)),
             dma((4, CHUNKS)),
             dma((1,)),
@@ -481,12 +485,15 @@
             dma((1,)),
             dma((NCTX,)),
             pltpu.SemaphoreType.REGULAR((ROUNDS + 1,)),
+            pltpu.VMEM((ROWS, GROUP * HD), BF16),
+            pltpu.SMEM((NDOCS,), jnp.int32),
+            pltpu.VMEM((NCTX, NCTX), jnp.int32),
         ],
         compiler_params=pltpu.CompilerParams(
             collective_id=0, has_side_effects=True, vmem_limit_bytes=60 * 1024 * 1024
         ),
         name="attend",
-    )(tokens, query, w_key, w_value, doc_lengths, balance, freq)
+    )(tokens, query, w_key, w_value, doc_lengths, balance)
 
 
 def solution(mesh):

time: 58.9 us -> 57.5 us (0.976)
  Pallas kernels: 56.4 us -> 55.6 us
  other arithmetic: 0.6 us -> 0 us
    pallas_call x1, Pallas kernels: 56.4 us -> 55.6 us  [local(): pl.pallas_call(kernel, out_shape=jax.ShapeDtypeStruct((ROWS, GROUP * HD),...]
    broadcast_in_dim x1 -> x0, other arithmetic: 0.59 us -> none  [local(): freq = jnp.concatenate([freq, freq])[None, :]]
where the time goes in v4:
time: 57.5 us; the launch traced here: 57.3 us
  Pallas kernels  55.6 us (97%)
  local copies, waits for them, and re-layouts  1.67 us (3%)
    pallas_call x1, Pallas kernels, local(): pl.pallas_call(kernel, out_shape=jax.ShapeDtypeStruct((ROWS, GROUP * HD),...  55.6 us
    unnamed x1, local copies, waits for them, and re-layouts  1.67 us

profile of v4, /device:TPU:1, one launch (start us, length us, event | category | flops | bytes accessed | tf_op | source)
XLA Modules:
  0.0 57.3 jit_solution(14590841400129282745)
XLA Ops:
  0.0 55.6 %attend.1 = bf16[256,512]{1,0:T(8,128)(2,1)} custom-call(bf16[256,1024]{1,0:T(8,128)(2,1)} %tokens.1, bf16[256,512]{1,0:T(8,128)(2,1)} %query.1, bf16[4096,128]{1,0:T(8,128)(2,1)} %w_key.1, bf16[4096,128]{1,0:T(8,128)(2,1)} %w_value.1, s32[16]{0:T(128)} %lengths_hbm.1, s32[32,32]{1,0:T(8,128)} %balance_hbm.1), custom_call_target="tpu_custom_call" | custom-call | tf_op jit(solution)/shard_map/attend/pallas_call | solution.py:457
  55.6 1.7 %copy.8 = bf16[256,512]{1,0:T(8,128)(2,1)} copy(bf16[256,512]{1,0:T(8,128)(2,1)} %attend.1) | data formatting | bytes 524288

commit v5 on v4

--- a/solution.py
+++ b/solution.py
@@ -304,9 +304,10 @@
         key = raw[:, HD:]
         key = key * cosf[rows, :] + pltpu.roll(key, HD // 2, 1) * sinf[rows, :]
         kv[OWN, rows, pl.ds(0, 2 * HD)] = jnp.concatenate([value, key], axis=1).astype(BF16)
-        for sign, count in ((1, FORWARD), (-1, BACKWARD)):
-            for h in range(1, count + 1):
-                hop_copy(c, sign, h).start()
+        for h in range(max(FORWARD, BACKWARD), 0, -1):
+            for sign, count in ((1, FORWARD), (-1, BACKWARD)):
+                if h <= count:
+                    hop_copy(c, sign, h).start()
 
     def gather(i, carry):
         for p in range(2):

time: 57.5 us -> 57 us (level)
  no operation moved by 1% of the time
where the time goes in v5:
time: 57 us; the launch traced here: 56.9 us
  Pallas kernels  55.2 us (97%)
  local copies, waits for them, and re-layouts  1.67 us (3%)
    pallas_call x1, Pallas kernels, local(): pl.pallas_call(kernel, out_shape=jax.ShapeDtypeStruct((ROWS, GROUP * HD),...  55.2 us
    unnamed x1, local copies, waits for them, and re-layouts  1.67 us

profile of v5, /device:TPU:1, one launch (start us, length us, event | category | flops | bytes accessed | tf_op | source)
XLA Modules:
  0.0 56.9 jit_solution(6164506076644288188)
XLA Ops:
  0.0 55.2 %attend.1 = bf16[256,512]{1,0:T(8,128)(2,1)} custom-call(bf16[256,1024]{1,0:T(8,128)(2,1)} %tokens.1, bf16[256,512]{1,0:T(8,128)(2,1)} %query.1, bf16[4096,128]{1,0:T(8,128)(2,1)} %w_key.1, bf16[4096,128]{1,0:T(8,128)(2,1)} %w_value.1, s32[16]{0:T(128)} %lengths_hbm.1, s32[32,32]{1,0:T(8,128)} %balance_hbm.1), custom_call_target="tpu_custom_call" | custom-call | tf_op jit(solution)/shard_map/attend/pallas_call | solution.py:458
  55.2 1.7 %copy.8 = bf16[256,512]{1,0:T(8,128)(2,1)} copy(bf16[256,512]{1,0:T(8,128)(2,1)} %attend.1) | data formatting | bytes 524288

commit v6 on v5

--- a/solution.py
+++ b/solution.py
@@ -356,8 +356,6 @@
         return carry
 
     lax.fori_loop(0, CHUNKS, gather, 0)
-    prepare_query()
-
     def finish_loop(c, carry):
         finish(c)
         return carry
@@ -365,6 +363,7 @@
     every = pl.ds(0, QROWS)
     lax.fori_loop(CHUNKS - LAG_OPP, CHUNKS - 1, finish_loop, 0)
     hops(0)
+    prepare_query()
     finish(CHUNKS - 1)
     hops(1)
     sib_arrived(0)

time: 57 us -> 57.2 us (level)
  no operation moved by 1% of the time
where the time goes in v6:
time: 57.2 us; the launch traced here: 57 us
  Pallas kernels  55.3 us (97%)
  local copies, waits for them, and re-layouts  1.67 us (3%)
    pallas_call x1, Pallas kernels, local(): pl.pallas_call(kernel, out_shape=jax.ShapeDtypeStruct((ROWS, GROUP * HD),...  55.3 us
    unnamed x1, local copies, waits for them, and re-layouts  1.67 us

profile of v6, /device:TPU:1, one launch (start us, length us, event | category | flops | bytes accessed | tf_op | source)
XLA Modules:
  0.0 57.0 jit_solution(16487813255376671671)
XLA Ops:
  0.0 55.3 %attend.1 = bf16[256,512]{1,0:T(8,128)(2,1)} custom-call(bf16[256,1024]{1,0:T(8,128)(2,1)} %tokens.1, bf16[256,512]{1,0:T(8,128)(2,1)} %query.1, bf16[4096,128]{1,0:T(8,128)(2,1)} %w_key.1, bf16[4096,128]{1,0:T(8,128)(2,1)} %w_value.1, s32[16]{0:T(128)} %lengths_hbm.1, s32[32,32]{1,0:T(8,128)} %balance_hbm.1), custom_call_target="tpu_custom_call" | custom-call | tf_op jit(solution)/shard_map/attend/pallas_call | solution.py:457
  55.3 1.7 %copy.8 = bf16[256,512]{1,0:T(8,128)(2,1)} copy(bf16[256,512]{1,0:T(8,128)(2,1)} %attend.1) | data formatting | bytes 524288
